TPU v7x, 256 devices: a whole 4x4x8 slice. The times are simulated.
256 devices in a mesh: gx: 16 (over x, z_hi), gy: 16 (over y, z_lo, core).
Axes of the slice: x: 4, y: 4, z: 8 (z_hi: 4, z_lo: 2; z = z_hi * 2 + z_lo), core: 2. Of those that a mesh axis runs over, the one named last changes fastest.
Arguments:
- in_field: float32 [1, 64, 128, 256], P(None, 'gx', 'gy'), may hold values from -6 to 6
- cotangent: float32 [1, 64, 128, 256], P(None, 'gx', 'gy'), may hold values from -6 to 6
- w_first: float32 [27, 8, 1], replicated, may hold values from -1.25 to 1.25
- w_down: float32 [16, 8, 2, 2, 2], replicated, may hold values from -0.75 to 0.75
- w_coarse: float32 [27, 16, 16], replicated, may hold values from -0.3125 to 0.3125
- w_up: float32 [8, 16, 2, 2, 2], replicated, may hold values from -1.5 to 1.5
- w_joined: float32 [27, 8, 16], replicated, may hold values from -0.3125 to 0.3125
- w_final: float32 [1, 8], replicated, may hold values from -2 to 2
Outputs:
- imitated: float32 [1, 64, 128, 256], P(None, 'gx', 'gy')
- grad_first: float32 [27, 8, 1], replicated
- grad_down: float32 [16, 8, 2, 2, 2], replicated
- grad_coarse: float32 [27, 16, 16], replicated
- grad_up: float32 [8, 16, 2, 2, 2], replicated
- grad_joined: float32 [27, 8, 16], replicated
- grad_final: float32 [1, 8], replicated
All inputs are finite; a program needn't handle non-finite values.
Results may differ from a plain program's by a relative error of at most 0.0003.
Values sent between devices are 32-bit elements; how exact they have to be, the bound alone decides.
No kernel may reach another device: no remote copies, remote signals or barrier semaphores. Data moves between devices by JAX's collectives and lax.ppermute only.
A program may use at most 128 MiB of HBM per device.

v0:
```python
import math

import jax
import jax.numpy as jnp
from jax import lax
from jax.experimental import pallas as pl
from jax.experimental.pallas import tpu as pltpu
from jax.sharding import PartitionSpec as P

F32 = jnp.float32
BF16 = jnp.bfloat16


def nn(a, b):
    return lax.dot_general(a, b, (((1,), (0,)), ((), ())), preferred_element_type=F32)


def nt(a, b):
    return lax.dot_general(a, b, (((1,), (1,)), ((), ())), preferred_element_type=F32)


def split(x):
    high = x.astype(BF16)
    return high, (x - high.astype(F32)).astype(BF16)


def rows(parts):
    return jnp.concatenate(parts, axis=0)


def lanes(parts):
    return jnp.concatenate(parts, axis=1)


def stacked(weight):
    return rows(list(split(weight)))


def mm3(both, high, low):
    count = both.shape[0] // 2
    first = nn(both, high)
    return first[:count] + first[count:] + nn(both[:count], low)


def nt3(left_high, left_low, right_high, right_low):
    count = left_high.shape[0]
    first = nt(rows([left_high, left_low]), right_high)
    return first[:count] + first[count:] + nt(left_high, right_low)


def thrice(base, depth):
    high, low = split(base)
    high = high.astype(F32)
    return high + roll(high, depth) + roll(low.astype(F32), 2 * depth)


def wider(base):
    return lanes([base, jnp.zeros((base.shape[0], 256 - base.shape[1]), F32)])


def roll(x, shift):
    shift = shift % x.shape[1]
    return x if shift == 0 else pltpu.roll(x, shift, 1)


def sigmoid(x):
    return 1.0 / (1.0 + jnp.exp(-x))


def lane_of(shape):
    return lax.broadcasted_iota(jnp.int32, shape, len(shape) - 1)


def back_one(x):
    return jnp.where(lane_of(x.shape) == 0, 0.0, pltpu.roll(x, 1, 1))


def ahead_one(x):
    return jnp.where(lane_of(x.shape) == 127, 0.0, pltpu.roll(x, 127, 1))


def four_depths(field):
    count = field.shape[0]
    even, odd = field[:, :8], field[:, 8:]
    before = back_one(odd.reshape(count * 8, 128)).reshape(count, 8, 128)
    after = ahead_one(even.reshape(count * 8, 128)).reshape(count, 8, 128)
    return jnp.concatenate([before, even, odd, after], axis=1)


def three_depths(field):
    count = field.shape[0]
    flat = field.reshape(count * 16, 128)
    return jnp.concatenate(
        [back_one(flat).reshape(count, 16, 128), field, ahead_one(flat).reshape(count, 16, 128)],
        axis=1,
    )


def inside(at, extent):
    return jnp.where((at >= 0) & (at < extent), 1.0, 0.0).astype(F32)


def plane_of(field, near, far, even_x, even_far):
    def plane(x):
        if 5 <= x < 9:
            return field[x - 5]
        pair, even, at = (far, even_far, 0) if x in (0, 13) else (near, even_x, x - 1 if x < 5 else x - 9)
        below = x < 5
        return jnp.where(even, pair[1 if below else 0][at], pair[0 if below else 1][at])

    return plane


def strips(pos, field, near_0, near_1, far_0, far_1, wide, out_0, out_1):
    px, py = pos[0], pos[1]
    even_y = (py & 1) == 0
    plane = plane_of(field, (near_0, near_1), (far_0, far_1), (px & 1) == 0, ((px >> 1) & 1) == 0)
    for x in range(14):
        own = plane(x)
        wide[x] = own
        low, high = own[0:5], own[3:8]
        out_0[5 * x : 5 * x + 5] = jnp.where(even_y, high, low)
        out_1[5 * x : 5 * x + 5] = jnp.where(even_y, low, high)


def run_strips(args):
    vmem = pl.BlockSpec(memory_space=pltpu.VMEM)
    return pl.pallas_call(
        strips,
        out_shape=tuple(jax.ShapeDtypeStruct(shape, F32) for shape in ((14, 8, 256), (70, 256), (70, 256))),
        in_specs=[pl.BlockSpec(memory_space=pltpu.SMEM)] + [vmem] * (len(args) - 1),
        out_specs=(vmem,) * 3,
        compiler_params=pltpu.CompilerParams(vmem_limit_bytes=4 * 1024 * 1024),
    )(*args)


def kernel(
    pos, wide, beside_0, beside_1, cot,
    b_first, b_down, b_down_t, b_coarse, b_coarse_t, b_up, b_up_t, b_joined, b_joined_t, wf_col,
    act_own, pay,
    fe, vh, vl, fh, fl, slope_f, pdh, pdl, slope_d, rc, slope_c, ch, cl, pjh, pjl, goh, gol,
    pgh, pgl, gdir, guh, gul, pch, pcl, gch, gcl, rd, gdh, gdl,
    *, scale, size_x, size_y,
):
    px, py = pos[0], pos[1]

    z = lax.broadcasted_iota(jnp.int32, (256, 512), 0)
    col = lane_of((256, 512))
    pick = jnp.where(z == 2 * (col & 127) + (col >> 7) - 1, 1.0, 0.0).astype(BF16)
    pick_two = pick[:, 128:384]

    even_y = (py & 1) == 0
    has_head, has_tail = inside(8 * py - 1, size_y), inside(8 * py + 8, size_y)
    for x in range(14):
        own = wide[x]
        first, second = beside_0[5 * x : 5 * x + 5], beside_1[5 * x : 5 * x + 5]
        head, tail = jnp.where(even_y, second, first), jnp.where(even_y, first, second)
        there = inside(4 * px + x - 5, size_x)
        head, own, tail = head * (there * has_head), own * there, tail * (there * has_tail)
        fe[x, 0] = rows([head, own, tail[0:3]])
        fe[x, 1] = rows([own[3:8], tail, jnp.zeros((6, 256), F32)])
    for source, target in zip(split(fe[...].reshape(448, 256)), (vh, vl)):
        found = nn(source, pick).astype(BF16)
        for v in range(4):
            target[:, :, 16 * v : 16 * v + 16, :] = found[:, 128 * v : 128 * v + 128].reshape(14, 2, 16, 128)

    def first_rhs(ref, at, window):
        return rows([lanes([ref[2 * at + a + dx, window] for a in range(2)]) for dx in range(3)])

    base = b_first[...]
    w_first = stacked(rows([roll(base, yo + 16 * c) for yo in range(8) for c in range(2)])[:, :192])
    row_y = (lax.broadcasted_iota(jnp.int32, (128, 256), 0) >> 4) + 8 * py - 4
    lane_a = lane_of((1, 256)) >> 7
    for at in range(6):
        mask_x = inside(4 * px + 2 * (at - 2) + lane_a, size_x)
        for window in range(2):
            mine = slice(128 * window, 128 * window + 128)
            pre = mm3(w_first, first_rhs(vh, at, window), first_rhs(vl, at, window))
            mask = inside(row_y + 8 * window, size_y) * mask_x
            sig = sigmoid(pre)
            act = pre * sig
            slope_f[at, mine] = (sig + act * (1.0 - sig)) * mask
            act = act * mask
            high, low = split(act)
            fh[at, mine] = high
            fl[at, mine] = low
            part = act.reshape(8, 16, 256)[2:8] if window == 0 else act.reshape(8, 16, 256)[0:6]
            for a in range(2):
                plane = 2 * (at - 1) + a - 1
                if 0 <= plane < 6:
                    half = slice(128 * (plane % 2), 128 * (plane % 2) + 128)
                    high, low = split(four_depths(part[:, :, 128 * a : 128 * a + 128]))
                    pjh[plane // 2, 6 * window : 6 * window + 6, 0:32, half] = high
                    pjl[plane // 2, 6 * window : 6 * window + 6, 0:32, half] = low

    base = b_down[...]
    w_down = stacked(rows([roll(base, 32 * k) for k in range(4)]))
    row_64 = lax.broadcasted_iota(jnp.int32, (64, 256), 0) >> 4
    for pair in range(3):
        mask_x = inside(2 * px + 2 * pair + lane_a - 2, size_x // 2)
        for y0 in (0, 4):
            def down_rhs(ref):
                return rows([
                    lanes([ref[2 * pair + j, 32 * y0 : 32 * y0 + 128, 128 * a : 128 * a + 128] for j in range(2)])
                    for a in range(2)
                ])
            pre = mm3(w_down, down_rhs(fh), down_rhs(fl))
            mask = inside(row_64 + y0 - 2 + 4 * py, size_y // 2) * mask_x
            sig = sigmoid(pre)
            act = pre * sig
            sloped = (sig + act * (1.0 - sig)) * mask
            act = act * mask
            for j in range(2):
                mine = slice(128 * j, 128 * j + 128)
                high, low = split(three_depths(act[:, mine].reshape(4, 16, 128)))
                pdh[2 * pair + j, y0 : y0 + 4] = high
                pdl[2 * pair + j, y0 : y0 + 4] = low
                slope_d[2 * pair + j, 16 * y0 : 16 * y0 + 64] = sloped[:, mine]

    base = b_coarse[...]
    w_coarse = stacked(
        rows([roll(base[16 * dx : 16 * dx + 16], 48 * k) for dx in range(3) for k in range(2)])[:, :192]
    )
    for pair in range(3):
        for k in range(3):
            def coarse_rhs(ref):
                return lanes([ref[2 * pair + j, 2 * k : 2 * k + 4].reshape(192, 128) for j in range(2)])
            part = mm3(w_coarse, coarse_rhs(pdh), coarse_rhs(pdl))
            for j in range(2):
                rc[2 * pair + j, k] = part[:, 128 * j : 128 * j + 128]
    row_32 = lax.broadcasted_iota(jnp.int32, (32, 128), 0) >> 4
    for at in range(4):
        mask_x = inside(2 * px + at - 1, size_x // 2)
        for k in range(3):
            mine = slice(32 * k, 32 * k + 32)
            pre = rc[at, k, 0:32] + rc[at + 1, k, 32:64] + rc[at + 2, k, 64:96]
            mask = inside(row_32 + 2 * k - 1 + 4 * py, size_y // 2) * mask_x
            sig = sigmoid(pre)
            act = pre * sig
            slope_c[at, mine] = (sig + act * (1.0 - sig)) * mask
            high, low = split(act * mask)
            ch[at, mine] = high
            cl[at, mine] = low

    base = b_up[...]
    base = thrice(wider(base), 48)
    w_up = rows([roll(base[32 * a : 32 * a + 32], 16 * k) for a in range(2) for k in range(3)])[:, :144].astype(BF16)
    for pair in range(2):
        for block in range(2):
            mine = slice(48 * block, 48 * block + 48)
            high = lanes([ch[2 * pair, mine], ch[2 * pair + 1, mine]])
            low = lanes([cl[2 * pair, mine], cl[2 * pair + 1, mine]])
            part = nn(w_up, rows([high, low, high]))
            for j in range(2):
                for a in range(2):
                    plane = 2 * (2 * pair + j) + a - 1
                    if 0 <= plane < 6:
                        half = slice(128 * (plane % 2), 128 * (plane % 2) + 128)
                        cells = part[96 * a : 96 * a + 96, 128 * j : 128 * j + 128].reshape(6, 16, 128)
                        high_part, low_part = split(four_depths(cells))
                        pjh[plane // 2, 6 * block : 6 * block + 6, 32:64, half] = high_part
                        pjl[plane // 2, 6 * block : 6 * block + 6, 32:64, half] = low_part

    found = nn(rows(list(split(cot[...].reshape(32, 256)))), pick_two)
    sel_row = lax.broadcasted_iota(jnp.int32, (128, 32), 0)
    sel_col = lane_of((128, 32)) & 15
    spread = jnp.where(sel_col == ((sel_row >> 3) & 1) * 8 + (sel_row >> 4), 1.0, 0.0).astype(BF16)
    cb = [
        nn(
            spread,
            rows([
                lanes([
                    found[32 * s + 16 * at + 8 * a : 32 * s + 16 * at + 8 * a + 8, 128 * c : 128 * c + 128]
                    for a in range(2)
                ])
                for s in range(2)
                for c in range(2)
            ]).astype(BF16),
        )
        for at in range(2)
    ]

    base = b_joined[...]
    w_joined = stacked(
        rows([
            roll(base[8 * dx : 8 * dx + 8], 64 * b + 8 * c) for dx in range(3) for b in range(2) for c in range(2)
        ])
    )
    wf_rows = wf_col[...] * scale
    for x in range(4):
        for ref in (pgh, pgl):
            ref[x, 0:3] = jnp.zeros((3, 32, 128), BF16)
            ref[x, 11:14] = jnp.zeros((3, 32, 128), BF16)

    def around_pair(ref, pair, k):
        return ref[pair, 2 * k + 1 : 2 * k + 5].reshape(256, 256)

    for k in range(4):
        part = [mm3(w_joined, around_pair(pjh, pair, k), around_pair(pjl, pair, k)) for pair in range(3)]
        for x in range(4):
            pre = sum(
                part[(x + dx) // 2][32 * dx : 32 * dx + 32, 128 * ((x + dx) % 2) : 128 * ((x + dx) % 2) + 128]
                for dx in range(3)
            )
            at, half = x // 2, slice(128 * (x % 2), 128 * (x % 2) + 128)
            mine = slice(32 * k, 32 * k + 32)
            sig = sigmoid(pre)
            act = pre * sig
            grad = cb[at][mine, half] * wf_rows * (sig + act * (1.0 - sig))
            high, low = split(four_depths(grad.reshape(2, 16, 128)))
            pgh[x, 2 * k + 3 : 2 * k + 5] = high
            pgl[x, 2 * k + 3 : 2 * k + 5] = low
            act_own[at, mine, half] = act
            high, low = split(grad)
            goh[x, mine] = high
            gol[x, mine] = low

    part_final = sum(jnp.sum((act_own[at] * cb[at]).reshape(16, 8, 256), axis=0) for at in range(2))
    part_final = jnp.sum(part_final, axis=1, keepdims=True) * scale

    nothing = jnp.zeros((32, 128), BF16)
    total = jnp.zeros((96, 256), F32)
    for pair in range(3):
        for k in range(4):
            def moved_rows(ref):
                return rows([
                    lanes([
                        ref[2 * pair + j - dx, 32 * k : 32 * k + 32] if 0 <= 2 * pair + j - dx < 4 else nothing
                        for j in range(2)
                    ])
                    for dx in range(3)
                ])
            total = total + nt3(
                moved_rows(goh), moved_rows(gol), around_pair(pjh, pair, k), around_pair(pjl, pair, k)
            )
    part_joined = rows([
        sum(
            roll(total[32 * dx + 16 * b + 8 * c : 32 * dx + 16 * b + 8 * c + 8], -(64 * b + 8 * c))
            for b in range(2)
            for c in range(2)
        )
        for dx in range(3)
    ])

    base = b_joined_t[...]
    w_back = stacked(
        rows([
            roll(base[8 * f : 8 * f + 8], 128 * a + 32 * b + 8 * c)
            for f in range(2)
            for a in range(2)
            for b in range(2)
            for c in range(2)
        ])
    )
    w_up_t = stacked(b_up_t[...][:, :64])
    for ref in (pch, pcl):
        for at in range(4):
            ref[at, 0:2] = jnp.zeros((2, 48, 128), BF16)
            ref[at, 8:10] = jnp.zeros((2, 48, 128), BF16)
    for at in range(4):
        planes = [(2 * at - 3 + xw, xw) for xw in range(4) if 0 <= 2 * at - 3 + xw < 4]
        weight = w_back[:, 128 * planes[0][1] : 128 * planes[-1][1] + 128]
        for pair in range(3):
            def back_rhs(ref):
                return rows([
                    lanes([ref[x, 4 * pair + 2 * j : 4 * pair + 2 * j + 4].reshape(128, 128) for j in range(2)])
                    for x, _ in planes
                ])
            result = mm3(weight, back_rhs(pgh), back_rhs(pgl))
            high, low = split(result[:64])
            grad_act = mm3(w_up_t, high, low)
            for j in range(2):
                cell = 2 * pair + j
                mine = slice(128 * j, 128 * j + 128)
                gdir[at, cell] = result[64:, mine]
                guh[at, 64 * cell : 64 * cell + 64] = high[:, mine]
                gul[at, 64 * cell : 64 * cell + 64] = low[:, mine]
                grad_pre = grad_act[:, mine] * slope_c[at, 16 * cell : 16 * cell + 16]
                part_high, part_low = split(three_depths(grad_pre.reshape(1, 16, 128)))
                pch[at, cell + 2] = part_high.reshape(48, 128)
                pcl[at, cell + 2] = part_low.reshape(48, 128)
                part_high, part_low = split(grad_pre)
                gch[at, 16 * cell : 16 * cell + 16] = part_high
                gcl[at, 16 * cell : 16 * cell + 16] = part_low

    total = jnp.zeros((384, 96), F32)
    for pair in range(2):
        def two(ref):
            return lanes([ref[2 * pair], ref[2 * pair + 1]])
        total = total + nt3(two(guh), two(gul), two(ch), two(cl))
    total = lanes([total, jnp.zeros((384, 32), F32)])
    part_up = sum(roll(total[64 * y : 64 * y + 64], -16 * y) for y in range(6))

    nothing = jnp.zeros((96, 128), BF16)
    total = jnp.zeros((288, 384), F32)
    for pair in range(3):
        def moved_cells(ref):
            return rows([
                lanes([ref[2 * pair + j - dx] if 0 <= 2 * pair + j - dx < 4 else nothing for j in range(2)])
                for dx in range(3)
            ])
        def plane_pair(ref):
            return lanes([ref[2 * pair + j].reshape(384, 128) for j in range(2)])
        total = total + nt3(moved_cells(gch), moved_cells(gcl), plane_pair(pdh), plane_pair(pdl))
    lane_512 = lane_of((1, 512))
    tap, chan = lane_512 & 31, lane_512 >> 5
    tap_y = (tap * 11) >> 5
    row_256 = lax.broadcasted_iota(jnp.int32, (256, 512), 0)
    to_taps = jnp.where(row_256 == jnp.where(tap < 9, 16 * tap + chan, -1), 1.0, 0.0).astype(BF16)
    parts = [
        sum(roll(total[96 * dx + 16 * y : 96 * dx + 16 * y + 16], -48 * y) for y in range(6))[:, 0:256]
        for dx in range(3)
    ]
    part_coarse = by_tap(parts, to_taps)
    key = 64 * tap_y + 32 * (chan >> 3) + 8 * (tap - 3 * tap_y) + (chan & 7)
    to_taps = jnp.where(row_256 == jnp.where(tap < 9, key, -1), 1.0, 0.0).astype(BF16)
    part_joined = by_tap([part_joined[8 * dx : 8 * dx + 8] for dx in range(3)], to_taps)

    base = b_coarse_t[...]
    w_back_coarse = stacked(
        rows([
            roll(base[:, 256 * dx : 256 * dx + 256], 48 * k) for dx in range(3) for k in range(2)
        ])[:, :192]
    )
    for pair in range(2):
        for k in range(4):
            def shifted(ref):
                return lanes([ref[2 * pair + j, 2 * k : 2 * k + 4].reshape(192, 128) for j in range(2)])
            part = mm3(w_back_coarse, shifted(pch), shifted(pcl))
            for j in range(2):
                rd[2 * pair + j, k] = part[:, 128 * j : 128 * j + 128]
    for at in range(6):
        for k in range(4):
            mine = slice(32 * k, 32 * k + 32)
            grad = sum(rd[at - 2 + dx, k, 32 * dx : 32 * dx + 32] for dx in range(3) if 0 <= at - 2 + dx < 4)
            high, low = split(grad * slope_d[at, mine])
            gdh[at, mine] = high
            gdl[at, mine] = low

    total = jnp.zeros((1024, 256), F32)
    for pair in range(3):
        def cells(ref):
            return lanes([ref[2 * pair], ref[2 * pair + 1]])
        def fine(ref):
            return rows([lanes([ref[2 * pair + j, :, 128 * a : 128 * a + 128] for j in range(2)]) for a in range(2)])
        total = total + nt(rows([fine(fh), fine(fl)]), rows([cells(gdh), cells(gdl)]))
    total = total[:512, :128] + total[:512, 128:] + total[512:, :128]
    part_down = rows([
        sum(roll(total[256 * a + 32 * y : 256 * a + 32 * y + 32], -16 * y) for y in range(8)) for a in range(2)
    ])

    base = b_down_t[...]
    base = thrice(wider(base), 64)
    w_back_down = rows([roll(base[32 * a : 32 * a + 32], 16 * k) for a in range(2) for k in range(4)])
    w_back_down = w_back_down[:, :192].astype(BF16)
    total = jnp.zeros((128, 256), F32)
    for pair in range(3):
        for window in range(2):
            mine = slice(64 * window, 64 * window + 64)
            high = lanes([gdh[2 * pair, mine], gdh[2 * pair + 1, mine]])
            low = lanes([gdl[2 * pair, mine], gdl[2 * pair + 1, mine]])
            back = nn(w_back_down, rows([high, low, high]))
            for j in range(2):
                at = 2 * pair + j
                halves = []
                for a in range(2):
                    half = back[128 * a : 128 * a + 128, 128 * j : 128 * j + 128]
                    if 1 <= at <= 4:
                        blocks = [
                            gdir[at - 1, y - 1, 32 * a : 32 * a + 32] if 1 <= y <= 6 else jnp.zeros((32, 128), F32)
                            for y in range(4 * window, 4 * window + 4)
                        ]
                        half = half + rows(blocks)
                    halves.append(half)
                high, low = split(lanes(halves) * slope_f[at, 128 * window : 128 * window + 128])
                pad = jnp.zeros((64, 256), BF16)
                total = total + nt3(
                    high, low, rows([first_rhs(vh, at, window), pad]), rows([first_rhs(vl, at, window), pad])
                )
    part_first = sum(
        roll(total[16 * y + 8 * c : 16 * y + 8 * c + 8], -(y + 16 * c)) for y in range(8) for c in range(2)
    )

    tap = lane_of((1, 128))
    tap_x = (tap * 57) >> 9
    tap_y = ((tap - 9 * tap_x) * 11) >> 5
    key = jnp.where(tap < 27, 64 * tap_x + 16 * (tap - 9 * tap_x - 3 * tap_y) + tap_y, -1)
    row_256 = lax.broadcasted_iota(jnp.int32, (256, 128), 0)
    part_first = exact(part_first, jnp.where(row_256 == key, 1.0, 0.0).astype(BF16))
    for m in range(4):
        pay[16 * m : 16 * m + 16] = part_coarse[:, 128 * m : 128 * m + 128]
        pay[64 + 8 * m : 72 + 8 * m] = part_joined[:, 128 * m : 128 * m + 128]
    lane = lane_of((16, 128))
    pay[96:112] = sum(
        roll(jnp.where(lane < 16, part[16 * m : 16 * m + 16], 0.0), 32 * m + at)
        for m in range(4)
        for part, at in ((part_down, 0), (part_up, 16))
    )
    lane, row = lane_of((8, 128)), lax.broadcasted_iota(jnp.int32, (8, 128), 0)
    pay[112:120] = part_first + jnp.where(lane == 64 + row, part_final, 0.0)


def image(act_own, wf_lanes, img):
    zt = lane_of((256, 256))
    rt = lax.broadcasted_iota(jnp.int32, (256, 256), 0)
    merge = jnp.where(zt == 2 * (rt & 127) + (rt >> 7), 1.0, 0.0).astype(BF16)
    f_row = lax.broadcasted_iota(jnp.int32, (16, 128), 0)
    f_col = lane_of((16, 128))
    w_final = stacked(
        jnp.where((f_row >> 3 == (f_col >> 3) & 1) & (f_row & 7 == f_col >> 4), wf_lanes[...], 0.0)
    )
    out_rows = []
    for at in range(2):
        result = mm3(w_final, *split(act_own[at]))
        for a in range(2):
            out_rows.append(lanes([result[8 * c : 8 * c + 8, 128 * a : 128 * a + 128] for c in range(2)]))
    whole = nn(stacked(rows(out_rows)), merge)
    img[...] = (whole[:32] + whole[32:]).reshape(4, 8, 256)


def run_image(act_own, wf_lanes):
    vmem = pl.BlockSpec(memory_space=pltpu.VMEM)
    return pl.pallas_call(
        image,
        out_shape=jax.ShapeDtypeStruct((4, 8, 256), F32),
        in_specs=[vmem, vmem],
        out_specs=vmem,
        compiler_params=pltpu.CompilerParams(vmem_limit_bytes=8 * 1024 * 1024),
        cost_estimate=pl.CostEstimate(flops=200_000_000, bytes_accessed=400_000, transcendentals=0),
    )(act_own, wf_lanes)


def exact(block, choice):
    high, low = split(block)
    rest = (block - high.astype(F32) - low.astype(F32)).astype(BF16)
    count = block.shape[0]
    found = nn(jnp.concatenate([high.astype(F32), low.astype(F32), rest.astype(F32)], axis=0).astype(BF16), choice)
    return found[:count] + found[count : 2 * count] + found[2 * count :]


def by_tap(parts, choice):
    count = parts[0].shape[0]
    found = exact(rows(parts), choice)
    return sum(roll(found[count * dx : count * dx + count], 9 * dx) for dx in range(len(parts)))


def outputs(*refs):
    blocks, (coarse, joined, first, down, up, final) = refs[:-6], refs[-6:]
    total = [ref[...] for ref in blocks]
    while len(total) > 1:
        total = [total[i] + total[i + 1] for i in range(0, len(total), 2)]
    total = total[0]

    def slot(start, count, at, width):
        block = total[start : start + count]
        return roll(block, -at)[:, :width]

    for i in range(16):
        coarse[:, i, :] = slot(16 * (i // 4), 16, 32 * (i % 4), 27)
        joined[:, i, :] = slot(64 + 8 * (i // 4), 8, 32 * (i % 4), 27)
    for k in range(8):
        down[:, k // 2, k % 2, :] = slot(96 + 8 * (k % 2), 8, 32 * (k // 2), 16)
        up[:, k // 2, k % 2, :] = slot(96 + 8 * (k % 2), 8, 32 * (k // 2) + 16, 16)
    first[:, 0, :] = total[112:120, :27]
    lane, row = lane_of((8, 128)), lax.broadcasted_iota(jnp.int32, (8, 128), 0)
    row_sum = jnp.sum(jnp.where(lane == 64 + row, total[112:120], 0.0), axis=0, keepdims=True)
    final[...] = roll(row_sum, -64)[:, :8]


def run_outputs(blocks):
    vmem = pl.BlockSpec(memory_space=pltpu.VMEM)
    shapes = ((16, 16, 27), (8, 16, 27), (8, 1, 27), (8, 4, 2, 16), (8, 4, 2, 16), (1, 8))
    return pl.pallas_call(
        outputs,
        out_shape=tuple(jax.ShapeDtypeStruct(shape, F32) for shape in shapes),
        in_specs=[vmem] * len(blocks),
        out_specs=(vmem,) * len(shapes),
        compiler_params=pltpu.CompilerParams(vmem_limit_bytes=4 * 1024 * 1024),
    )(*blocks)


def run_kernel(args, scale, size_x, size_y):
    vmem = pl.BlockSpec(memory_space=pltpu.VMEM)

    def pair(*shape):
        return [pltpu.VMEM(shape, BF16)] * 2

    def plain(*shape):
        return [pltpu.VMEM(shape, F32)]

    scratch = (
        plain(14, 2, 16, 256)
        + pair(14, 2, 64, 128)
        + pair(6, 256, 256)
        + plain(6, 256, 256)
        + pair(6, 8, 48, 128)
        + plain(6, 128, 128)
        + plain(6, 3, 96, 128)
        + plain(4, 96, 128)
        + pair(4, 96, 128)
        + pair(3, 12, 64, 256)
        + pair(4, 128, 128)
        + pair(4, 14, 32, 128)
        + plain(4, 6, 64, 128)
        + pair(4, 384, 128)
        + pair(4, 10, 48, 128)
        + pair(4, 96, 128)
        + plain(4, 4, 96, 128)
        + pair(6, 128, 128)
    )

    def unet_tile(*refs):
        kernel(*refs, scale=scale, size_x=size_x, size_y=size_y)

    return pl.pallas_call(
        unet_tile,
        out_shape=(jax.ShapeDtypeStruct((2, 128, 256), F32), jax.ShapeDtypeStruct((120, 128), F32)),
        in_specs=[pl.BlockSpec(memory_space=pltpu.SMEM)] + [vmem] * (len(args) - 1),
        out_specs=(vmem, vmem),
        scratch_shapes=scratch,
        compiler_params=pltpu.CompilerParams(vmem_limit_bytes=48 * 1024 * 1024),
        cost_estimate=pl.CostEstimate(flops=3_000_000_000, bytes_accessed=2_000_000, transcendentals=2_000_000),
    )(*args)


def swap(first, second, axis, by):
    count = lax.axis_size(axis)

    def pairs(parity):
        return [(i, (i + (by if (i // by) % 2 == parity else -by)) % count) for i in range(count)]

    return lax.ppermute(first, axis, pairs(0)), lax.ppermute(second, axis, pairs(1))


def rounds(count, apart):
    groups = [[k * by for k in (1, 2, 3) if k * by < count] for by in (1, 4, 16, 64) if by < count]
    if apart and len(groups[0]) == 3:
        groups = [[1], [3]] + groups[1:]
    return groups


def padded(block, *shape):
    return jnp.pad(block, [(0, want - have) for want, have in zip(shape, block.shape)])


def bases_now(w_first, w_joined, w_final):
    first = w_first.reshape(3, 3, 3, 8).transpose(3, 0, 2, 1)
    first = padded(first, 8, 4, 4, 16).reshape(8, 256)
    joined = w_joined.reshape(3, 3, 3, 8, 2, 8)
    joined_out = padded(joined.transpose(0, 3, 1, 4, 2, 5), 3, 8, 4, 2, 4, 8).reshape(24, 256)
    joined_t = joined[::-1, ::-1, ::-1, :, ::-1].transpose(4, 5, 0, 1, 2, 3)
    joined_t = padded(joined_t, 2, 8, 4, 4, 4, 8).reshape(16, 512)
    wf_lanes = jnp.tile(w_final, (1, 16))
    wf_col = jnp.tile(w_final.reshape(8, 1), (4, 1))
    return first, joined_out, joined_t, wf_lanes, wf_col


def bases_later(w_down, w_coarse, w_up):
    down = padded(w_down.transpose(0, 2, 3, 4, 1).reshape(16, 2, 32), 16, 2, 128).reshape(16, 256)
    down_t = padded(w_down.transpose(2, 3, 4, 1, 0).reshape(64, 16), 64, 128)
    coarse = w_coarse.reshape(3, 3, 3, 16, 16)
    coarse_out = padded(coarse.transpose(0, 3, 1, 2, 4).reshape(48, 144), 48, 256)
    coarse_t = coarse[::-1, ::-1, ::-1].transpose(4, 0, 1, 2, 3).reshape(16, 3, 144)
    coarse_t = padded(coarse_t, 16, 3, 256).reshape(16, 768)
    up = padded(w_up.transpose(2, 3, 4, 0, 1).reshape(64, 16), 64, 128)
    up_t = padded(w_up.transpose(1, 2, 3, 4, 0).reshape(16, 64), 16, 128)
    return down, down_t, coarse_out, coarse_t, up, up_t


def shards(in_field, cotangent, w_first, w_down, w_coarse, w_up, w_joined, w_final):
    size_x, size_y = 4 * lax.axis_size("gx"), 8 * lax.axis_size("gy")
    field, cot = in_field[0], cotangent[0]
    now = bases_now(w_first, w_joined, w_final)
    pos = jnp.stack([lax.axis_index("gx"), lax.axis_index("gy")]).astype(jnp.int32)
    even = ((lax.axis_index("gx") >> 1) & 1) == 0
    low, high = field[:1], field[3:]
    far = swap(jnp.where(even, high, low), jnp.where(even, low, high), "gx", 2)
    near = swap(field, field, "gx", 1)
    near, far, now, pos, (w_down, w_coarse, w_up) = lax.optimization_barrier(
        (near, far, now, pos, (w_down, w_coarse, w_up))
    )
    wide, *sent = run_strips([pos, field, *near, *far])
    beside = swap(*sent, "gy", 1)
    first, joined_out, joined_t, wf_lanes, wf_col = now
    later = bases_later(w_down, w_coarse, w_up)
    weights = [first, *later, joined_out, joined_t, wf_col]

    scale = 1.0 / math.sqrt(size_x * size_y * in_field.shape[3])
    act_own, pay = run_kernel([pos, wide, *beside, cot, *weights], scale, size_x, size_y)

    blocks, imitated = [pay], None
    for axis in ("gy", "gx"):
        count = lax.axis_size(axis)
        for partners in rounds(count, axis == "gx"):
            while len(blocks) > 1:
                blocks = [blocks[i] + blocks[i + 1] for i in range(0, len(blocks), 2)]
            mine = blocks[0]
            blocks = [mine] + [lax.ppermute(mine, axis, [(i, i ^ k) for i in range(count)]) for k in partners]
            if imitated is None:
                act_own, blocks = lax.optimization_barrier((act_own, blocks))
                imitated = run_image(act_own, wf_lanes)
    coarse, joined, first, down, up, final = run_outputs(blocks)
    return (
        imitated[None],
        first.transpose(2, 0, 1),
        down.reshape(8, 2, 2, 2, 16).transpose(4, 0, 1, 2, 3),
        coarse.transpose(2, 0, 1),
        up.reshape(8, 2, 2, 2, 16).transpose(0, 4, 1, 2, 3),
        joined.transpose(2, 0, 1),
        final,
    )


def solution(mesh):
    in_specs = (P(None, "gx", "gy", None), P(None, "gx", "gy", None), P(), P(), P(), P(), P(), P())
    out_specs = (P(None, "gx", "gy", None), P(), P(), P(), P(), P(), P())
    return jax.shard_map(shards, mesh=mesh, in_specs=in_specs, out_specs=out_specs, check_vma=False)
```

profile of v0, /device:TPU:6, one launch (start us, length us, event | category | flops | bytes accessed | tf_op | source)
XLA Modules:
  0.0 74.4 jit_solution(9234409553694484097)
XLA Ops:
  0.6 3.4 %collective-permute-start = (f32[4,8,256]{2,1,0:T(8,128)}, f32[4,8,256]{2,1,0:T(8,128)S(1)}, u32[]{:S(2)}, u32[]{:S(2)}) collective-permute-start(f32[4,8,256]{2,1,0:T(8,128)} %bitcast.43), channel_id=1, source_target_pairs={{0,16},{16,0},{32,48},{48,32},{64,80},{80,64},{96,112},{112,96},{1... | collective-permute-start | bytes 98312 | tf_op jit(solution)/shard_map/ppermute | solution.py:632
  4.0 4.7 %collective-permute-start.1 = (f32[4,8,256]{2,1,0:T(8,128)}, f32[4,8,256]{2,1,0:T(8,128)S(1)}, u32[]{:S(2)}, u32[]{:S(2)}) collective-permute-start(f32[4,8,256]{2,1,0:T(8,128)} %bitcast.44), channel_id=1, source_target_pairs={{0,240},{16,32},{32,16},{48,64},{64,48},{80,96},{96,80},{112,128},... | collective-permute-start | bytes 98312 | tf_op jit(solution)/shard_map/ppermute | solution.py:632
  8.7 0.7 select_bitcast_fusion
  9.5 0.7 collective-permute-start.2
  10.2 5.2 %collective-permute-start.3 = (f32[1,8,256]{2,1,0:T(8,128)S(1)}, f32[1,8,256]{2,1,0:T(8,128)S(1)}, u32[]{:S(2)}, u32[]{:S(2)}) collective-permute-start(f32[1,8,256]{2,1,0:T(8,128)S(1)} %get-tuple-element.65), channel_id=1, source_target_pairs={{0,224},{16,240},{32,64},{48,80},{64,32},{80,48},{96,128},{112,144... | collective-permute-start | bytes 24584 | tf_op jit(solution)/shard_map/ppermute | solution.py:632
  15.4 0.1 pad_add_fusion.pos.refs_0_
  15.5 0.6 copy-done.6
  16.1 0.1 copy.24
  16.2 0.2 copy.43
  16.3 0.0 copy-start.5
  16.3 0.1 reshape.121.refs_5_
  16.5 0.7 copy-done.5
  17.2 0.1 copy.26
  17.3 0.2 reshape.122
  17.5 0.5 rev.6
  18.0 0.1 copy.44
  18.2 0.1 pad.36.clone
  18.3 0.4 reshape.123.refs_12_
  18.6 0.2 pad.37
  18.8 0.3 reshape.136
  19.1 0.0 copy-start
  19.2 0.1 copy.40.refs_13_
  19.3 0.7 copy-done.7
  19.9 0.1 tile.21.wf_lanes
  20.0 0.1 tile.23
  20.1 0.6 shard_map.135
  20.7 0.1 collective-permute-start.4
  20.8 3.6 %collective-permute-start.5 = (f32[70,256]{1,0:T(8,128)S(1)}, f32[70,256]{1,0:T(8,128)S(1)}, u32[]{:S(2)}, u32[]{:S(2)}) collective-permute-start(f32[70,256]{1,0:T(8,128)S(1)} %get-tuple-element.43), channel_id=1, source_target_pairs={{0,15},{1,2},{2,1},{3,4},{4,3},{5,6},{6,5},{7,8},{8,7},{9,10},{10,... | collective-permute-start | bytes 215048 | tf_op jit(solution)/shard_map/ppermute | solution.py:632
  24.4 0.0 copy-start.4
  24.4 0.1 copy.41.refs_6_
  24.5 0.8 %copy-done.4 = f32[27,16,16]{0,2,1:T(8,128)S(1)} copy-done((f32[27,16,16]{0,2,1:T(8,128)S(1)}, f32[27,16,16]{0,2,1:T(8,128)}, u32[]{:S(2)}) %copy-start.4) | copy-done | bytes 27672
  25.3 0.2 copy.32
  25.5 0.1 copy.33
  25.6 0.2 reshape.129
  25.8 0.2 copy.45
  26.1 0.7 copy-done.3
  26.8 0.0 copy-start.1
  26.8 0.1 copy.38
  26.9 0.1 copy.39.refs_14_
  27.0 0.1 collective-permute-done.5.refs_3_
  27.1 0.5 copy-done.1
  27.6 10.8 %shard_map.136 = (f32[2,128,256]{2,1,0:T(8,128)S(1)}, f32[120,128]{1,0:T(8,128)S(1)}) custom-call(s32[2]{0:T(128)S(1)} %pad_add_fusion.pos.refs_0_, f32[14,8,256]{2,1,0:T(8,128)S(1)} %get-tuple-element.41.refs_1_, f32[70,256]{1,0:T(8,128)S(1)} %collective-permute-done.4.refs_2_, f32[70,256]{1,0:T(8,128)S(1)} %collective-permute-done.5.refs_3_, ...), custom_call_target="tpu_custom_call" | custom-call | flops 3000000000 | bytes 2000000 | tf_op jit(solution)/shard_map/pallas_call | solution.py:615
  38.4 0.1 collective-permute-start.6
  38.5 0.1 collective-permute-start.7
  38.6 1.8 %collective-permute-start.8 = (f32[120,128]{1,0:T(8,128)S(1)}, f32[120,128]{1,0:T(8,128)S(1)}, u32[]{:S(2)}, u32[]{:S(2)}) collective-permute-start(f32[120,128]{1,0:T(8,128)S(1)} %get-tuple-element.55), channel_id=1, source_target_pairs={{0,3},{1,2},{2,1},{3,0},{4,7},{5,6},{6,5},{7,4},{8,11},{9,10},{10,... | collective-permute-start | bytes 184328 | tf_op jit(solution)/shard_map/ppermute | solution.py:698
  40.4 3.0 %collective-permute-done.7 = f32[120,128]{1,0:T(8,128)S(1)} collective-permute-done((f32[120,128]{1,0:T(8,128)S(1)}, f32[120,128]{1,0:T(8,128)S(1)}, u32[]{:S(2)}, u32[]{:S(2)}) %collective-permute-start.7) | collective-permute-done | bytes 61472 | tf_op jit(solution)/shard_map/ppermute | solution.py:698
  43.4 0.4 collective-permute-done.8
  43.8 1.9 %collective-permute-start.10 = (f32[120,128]{1,0:T(8,128)S(1)}, f32[120,128]{1,0:T(8,128)S(1)}, u32[]{:S(2)}, u32[]{:S(2)}) collective-permute-start(f32[120,128]{1,0:T(8,128)S(1)} %add_add_fusion.1), channel_id=1, source_target_pairs={{0,8},{1,9},{2,10},{3,11},{4,12},{5,13},{6,14},{7,15},{8,0},{9,1},... | collective-permute-start | bytes 184328 | tf_op jit(solution)/shard_map/ppermute | solution.py:698
  45.7 1.4 %collective-permute-start.11 = (f32[120,128]{1,0:T(8,128)S(1)}, f32[120,128]{1,0:T(8,128)S(1)}, u32[]{:S(2)}, u32[]{:S(2)}) collective-permute-start(f32[120,128]{1,0:T(8,128)S(1)} %add_add_fusion.1), channel_id=1, source_target_pairs={{0,12},{1,13},{2,14},{3,15},{4,8},{5,9},{6,10},{7,11},{8,4},{9,5},... | collective-permute-start | bytes 184328 | tf_op jit(solution)/shard_map/ppermute | solution.py:698
  47.1 0.3 collective-permute-start.9
  47.4 2.2 %collective-permute-done.10 = f32[120,128]{1,0:T(8,128)S(1)} collective-permute-done((f32[120,128]{1,0:T(8,128)S(1)}, f32[120,128]{1,0:T(8,128)S(1)}, u32[]{:S(2)}, u32[]{:S(2)}) %collective-permute-start.10) | collective-permute-done | bytes 61472 | tf_op jit(solution)/shard_map/ppermute | solution.py:698
  49.6 1.5 %collective-permute-done.11 = f32[120,128]{1,0:T(8,128)S(1)} collective-permute-done((f32[120,128]{1,0:T(8,128)S(1)}, f32[120,128]{1,0:T(8,128)S(1)}, u32[]{:S(2)}, u32[]{:S(2)}) %collective-permute-start.11) | collective-permute-done | bytes 61472 | tf_op jit(solution)/shard_map/ppermute | solution.py:698
  51.1 0.2 collective-permute-done.9
  51.3 1.8 %collective-permute-start.12 = (f32[120,128]{1,0:T(8,128)S(1)}, f32[120,128]{1,0:T(8,128)S(1)}, u32[]{:S(2)}, u32[]{:S(2)}) collective-permute-start(f32[120,128]{1,0:T(8,128)S(1)} %add_add_fusion), channel_id=1, source_target_pairs={{0,16},{16,0},{32,48},{48,32},{64,80},{80,64},{96,112},{112,96},{1... | collective-permute-start | bytes 184328 | tf_op jit(solution)/shard_map/ppermute | solution.py:698
  53.1 4.3 %collective-permute-done.12 = f32[120,128]{1,0:T(8,128)S(1)} collective-permute-done((f32[120,128]{1,0:T(8,128)S(1)}, f32[120,128]{1,0:T(8,128)S(1)}, u32[]{:S(2)}, u32[]{:S(2)}) %collective-permute-start.12) | collective-permute-done | bytes 61472 | tf_op jit(solution)/shard_map/ppermute | solution.py:698
  57.4 3.2 %collective-permute-start.13 = (f32[120,128]{1,0:T(8,128)S(1)}, f32[120,128]{1,0:T(8,128)S(1)}, u32[]{:S(2)}, u32[]{:S(2)}) collective-permute-start(f32[120,128]{1,0:T(8,128)S(1)} %add.48), channel_id=1, source_target_pairs={{0,48},{16,32},{32,16},{48,0},{64,112},{80,96},{96,80},{112,64},{1... | collective-permute-start | bytes 184328 | tf_op jit(solution)/shard_map/ppermute | solution.py:698
  60.7 3.2 %collective-permute-done.13 = f32[120,128]{1,0:T(8,128)S(1)} collective-permute-done((f32[120,128]{1,0:T(8,128)S(1)}, f32[120,128]{1,0:T(8,128)S(1)}, u32[]{:S(2)}, u32[]{:S(2)}) %collective-permute-start.13) | collective-permute-done | bytes 61472 | tf_op jit(solution)/shard_map/ppermute | solution.py:698
  63.9 0.6 collective-permute-start.14
  64.5 3.6 %collective-permute-start.15 = (f32[120,128]{1,0:T(8,128)S(1)}, f32[120,128]{1,0:T(8,128)S(1)}, u32[]{:S(2)}, u32[]{:S(2)}) collective-permute-start(f32[120,128]{1,0:T(8,128)S(1)} %add.49.refs_0_), channel_id=1, source_target_pairs={{0,128},{16,144},{32,160},{48,176},{64,192},{80,208},{96,224},{112... | collective-permute-start | bytes 184328 | tf_op jit(solution)/shard_map/ppermute | solution.py:698
  68.1 0.5 collective-permute-start.16
  68.6 0.9 %shard_map.137 = f32[4,8,256]{2,1,0:T(8,128)} custom-call(f32[2,128,256]{2,1,0:T(8,128)S(1)} %get-tuple-element.53.act_own, f32[1,128]{1,0:T(1,128)S(1)} %tile.21.wf_lanes), custom_call_target="tpu_custom_call" | custom-call | flops 200000000 | bytes 400000 | tf_op jit(solution)/shard_map/pallas_call | solution.py:523
  69.6 1.4 %collective-permute-done.15.refs_2_ = f32[120,128]{1,0:T(8,128)S(1)} collective-permute-done((f32[120,128]{1,0:T(8,128)S(1)}, f32[120,128]{1,0:T(8,128)S(1)}, u32[]{:S(2)}, u32[]{:S(2)}) %collective-permute-start.15) | collective-permute-done | bytes 61472 | tf_op jit(solution)/shard_map/ppermute | solution.py:698
  71.0 2.6 %collective-permute-done.16.refs_3_ = f32[120,128]{1,0:T(8,128)S(1)} collective-permute-done((f32[120,128]{1,0:T(8,128)S(1)}, f32[120,128]{1,0:T(8,128)S(1)}, u32[]{:S(2)}, u32[]{:S(2)}) %collective-permute-start.16) | collective-permute-done | bytes 61472 | tf_op jit(solution)/shard_map/ppermute | solution.py:698
  73.6 0.8 %shard_map.138 = (f32[16,16,27]{2,1,0:T(8,128)}, f32[8,16,27]{2,1,0:T(8,128)}, f32[8,1,27]{2,1,0:T(1,128)}, f32[8,4,2,16]{3,2,1,0:T(2,128)}, f32[8,4,2,16]{3,2,1,0:T(2,128)}, /*index=5*/f32[1,8]{1,0:T(1,128)}) custom-call(f32[120,128]{1,0:T(8,128)S(1)} %add.49.refs_0_, f32[120,128]{1,0:T(8,128)S(1)} %collective-permute-done.14.refs_1_, ...), custom_call_target="tpu_custom_call" | custom-call | tf_op jit(solution)/shard_map/pallas_call | solution.py:573
  (33 shorter events, 0.2 us)
Async XLA Ops:
  0.6 19.5 %collective-permute-start = (f32[4,8,256]{2,1,0:T(8,128)}, f32[4,8,256]{2,1,0:T(8,128)S(1)}, u32[]{:S(2)}, u32[]{:S(2)}) collective-permute-start(f32[4,8,256]{2,1,0:T(8,128)} %bitcast.43), channel_id=1, source_target_pairs={{0,16},{16,0},{32,48},{48,32},{64,80},{80,64},{96,112},{112,96},{1... | collective-permute-start | bytes 98312 | tf_op jit(solution)/shard_map/ppermute | solution.py:632
  4.0 16.1 %collective-permute-start.1 = (f32[4,8,256]{2,1,0:T(8,128)}, f32[4,8,256]{2,1,0:T(8,128)S(1)}, u32[]{:S(2)}, u32[]{:S(2)}) collective-permute-start(f32[4,8,256]{2,1,0:T(8,128)} %bitcast.44), channel_id=1, source_target_pairs={{0,240},{16,32},{32,16},{48,64},{64,48},{80,96},{96,80},{112,128},... | collective-permute-start | bytes 98312 | tf_op jit(solution)/shard_map/ppermute | solution.py:632
  9.5 10.6 %collective-permute-start.2 = (f32[1,8,256]{2,1,0:T(8,128)S(1)}, f32[1,8,256]{2,1,0:T(8,128)S(1)}, u32[]{:S(2)}, u32[]{:S(2)}) collective-permute-start(f32[1,8,256]{2,1,0:T(8,128)S(1)} %get-tuple-element.66), channel_id=1, source_target_pairs={{0,32},{16,48},{32,0},{48,16},{64,96},{80,112},{96,64},{112,80},{1... | collective-permute-start | bytes 24584 | tf_op jit(solution)/shard_map/ppermute | solution.py:632
  10.2 10.0 %collective-permute-start.3 = (f32[1,8,256]{2,1,0:T(8,128)S(1)}, f32[1,8,256]{2,1,0:T(8,128)S(1)}, u32[]{:S(2)}, u32[]{:S(2)}) collective-permute-start(f32[1,8,256]{2,1,0:T(8,128)S(1)} %get-tuple-element.65), channel_id=1, source_target_pairs={{0,224},{16,240},{32,64},{48,80},{64,32},{80,48},{96,128},{112,144... | collective-permute-start | bytes 24584 | tf_op jit(solution)/shard_map/ppermute | solution.py:632
  15.4 0.7 copy-start.6
  16.3 0.8 %copy-start.5 = (f32[27,8,16]{0,2,1:T(8,128)S(1)}, f32[27,8,16]{0,2,1:T(8,128)}, u32[]{:S(2)}) copy-start(f32[27,8,16]{0,2,1:T(8,128)} %param.14) | copy-start | bytes 41476
  19.1 1.0 %copy-start = (f32[1,4,8,256]{3,2,1,0:T(8,128)S(1)}, f32[1,4,8,256]{3,2,1,0:T(8,128)}, u32[]{:S(2)}) copy-start(f32[1,4,8,256]{3,2,1,0:T(8,128)} %param.8) | copy-start | bytes 98308
  19.2 0.7 copy-start.7
  20.1 4.3 %copy-start.2 = (f32[16,8,2,2,2]{0,4,3,2,1:T(2,128)S(1)}, f32[16,8,2,2,2]{0,4,3,2,1:T(2,128)}, u32[]{:S(2)}) copy-start(f32[16,8,2,2,2]{0,4,3,2,1:T(2,128)} %param.11) | copy-start | bytes 12292
  20.7 6.3 %collective-permute-start.4 = (f32[70,256]{1,0:T(8,128)S(1)}, f32[70,256]{1,0:T(8,128)S(1)}, u32[]{:S(2)}, u32[]{:S(2)}) collective-permute-start(f32[70,256]{1,0:T(8,128)S(1)} %get-tuple-element.42), channel_id=1, source_target_pairs={{0,1},{1,0},{2,3},{3,2},{4,5},{5,4},{6,7},{7,6},{8,9},{9,8},{10,11... | collective-permute-start | bytes 215048 | tf_op jit(solution)/shard_map/ppermute | solution.py:632
  20.8 6.2 %collective-permute-start.5 = (f32[70,256]{1,0:T(8,128)S(1)}, f32[70,256]{1,0:T(8,128)S(1)}, u32[]{:S(2)}, u32[]{:S(2)}) collective-permute-start(f32[70,256]{1,0:T(8,128)S(1)} %get-tuple-element.43), channel_id=1, source_target_pairs={{0,15},{1,2},{2,1},{3,4},{4,3},{5,6},{6,5},{7,8},{8,7},{9,10},{10,... | collective-permute-start | bytes 215048 | tf_op jit(solution)/shard_map/ppermute | solution.py:632
  24.4 0.9 %copy-start.4 = (f32[27,16,16]{0,2,1:T(8,128)S(1)}, f32[27,16,16]{0,2,1:T(8,128)}, u32[]{:S(2)}) copy-start(f32[27,16,16]{0,2,1:T(8,128)} %param.12) | copy-start | bytes 82948
  26.0 0.8 %copy-start.3 = (f32[8,16,2,2,2]{1,4,3,2,0:T(2,128)S(1)}, f32[8,16,2,2,2]{1,4,3,2,0:T(2,128)}, u32[]{:S(2)}) copy-start(f32[8,16,2,2,2]{1,4,3,2,0:T(2,128)} %param.13) | copy-start | bytes 12292
  26.8 0.8 %copy-start.1 = (f32[1,4,8,256]{3,2,1,0:T(8,128)S(1)}, f32[1,4,8,256]{3,2,1,0:T(8,128)}, u32[]{:S(2)}) copy-start(f32[1,4,8,256]{3,2,1,0:T(8,128)} %param.9) | copy-start | bytes 98308
  38.4 2.0 %collective-permute-start.6 = (f32[120,128]{1,0:T(8,128)S(1)}, f32[120,128]{1,0:T(8,128)S(1)}, u32[]{:S(2)}, u32[]{:S(2)}) collective-permute-start(f32[120,128]{1,0:T(8,128)S(1)} %get-tuple-element.55), channel_id=1, source_target_pairs={{0,1},{1,0},{2,3},{3,2},{4,5},{5,4},{6,7},{7,6},{8,9},{9,8},{10,11... | collective-permute-start | bytes 184328 | tf_op jit(solution)/shard_map/ppermute | solution.py:698
  38.5 4.9 %collective-permute-start.7 = (f32[120,128]{1,0:T(8,128)S(1)}, f32[120,128]{1,0:T(8,128)S(1)}, u32[]{:S(2)}, u32[]{:S(2)}) collective-permute-start(f32[120,128]{1,0:T(8,128)S(1)} %get-tuple-element.55), channel_id=1, source_target_pairs={{0,2},{1,3},{2,0},{3,1},{4,6},{5,7},{6,4},{7,5},{8,10},{9,11},{10,... | collective-permute-start | bytes 184328 | tf_op jit(solution)/shard_map/ppermute | solution.py:698
  38.6 5.2 %collective-permute-start.8 = (f32[120,128]{1,0:T(8,128)S(1)}, f32[120,128]{1,0:T(8,128)S(1)}, u32[]{:S(2)}, u32[]{:S(2)}) collective-permute-start(f32[120,128]{1,0:T(8,128)S(1)} %get-tuple-element.55), channel_id=1, source_target_pairs={{0,3},{1,2},{2,1},{3,0},{4,7},{5,6},{6,5},{7,4},{8,11},{9,10},{10,... | collective-permute-start | bytes 184328 | tf_op jit(solution)/shard_map/ppermute | solution.py:698
  43.8 5.8 %collective-permute-start.10 = (f32[120,128]{1,0:T(8,128)S(1)}, f32[120,128]{1,0:T(8,128)S(1)}, u32[]{:S(2)}, u32[]{:S(2)}) collective-permute-start(f32[120,128]{1,0:T(8,128)S(1)} %add_add_fusion.1), channel_id=1, source_target_pairs={{0,8},{1,9},{2,10},{3,11},{4,12},{5,13},{6,14},{7,15},{8,0},{9,1},... | collective-permute-start | bytes 184328 | tf_op jit(solution)/shard_map/ppermute | solution.py:698
  45.7 5.4 %collective-permute-start.11 = (f32[120,128]{1,0:T(8,128)S(1)}, f32[120,128]{1,0:T(8,128)S(1)}, u32[]{:S(2)}, u32[]{:S(2)}) collective-permute-start(f32[120,128]{1,0:T(8,128)S(1)} %add_add_fusion.1), channel_id=1, source_target_pairs={{0,12},{1,13},{2,14},{3,15},{4,8},{5,9},{6,10},{7,11},{8,4},{9,5},... | collective-permute-start | bytes 184328 | tf_op jit(solution)/shard_map/ppermute | solution.py:698
  47.1 4.2 %collective-permute-start.9 = (f32[120,128]{1,0:T(8,128)S(1)}, f32[120,128]{1,0:T(8,128)S(1)}, u32[]{:S(2)}, u32[]{:S(2)}) collective-permute-start(f32[120,128]{1,0:T(8,128)S(1)} %add_add_fusion.1), channel_id=1, source_target_pairs={{0,4},{1,5},{2,6},{3,7},{4,0},{5,1},{6,2},{7,3},{8,12},{9,13},{10,... | collective-permute-start | bytes 184328 | tf_op jit(solution)/shard_map/ppermute | solution.py:698
  51.3 6.1 %collective-permute-start.12 = (f32[120,128]{1,0:T(8,128)S(1)}, f32[120,128]{1,0:T(8,128)S(1)}, u32[]{:S(2)}, u32[]{:S(2)}) collective-permute-start(f32[120,128]{1,0:T(8,128)S(1)} %add_add_fusion), channel_id=1, source_target_pairs={{0,16},{16,0},{32,48},{48,32},{64,80},{80,64},{96,112},{112,96},{1... | collective-permute-start | bytes 184328 | tf_op jit(solution)/shard_map/ppermute | solution.py:698
  57.4 6.4 %collective-permute-start.13 = (f32[120,128]{1,0:T(8,128)S(1)}, f32[120,128]{1,0:T(8,128)S(1)}, u32[]{:S(2)}, u32[]{:S(2)}) collective-permute-start(f32[120,128]{1,0:T(8,128)S(1)} %add.48), channel_id=1, source_target_pairs={{0,48},{16,32},{32,16},{48,0},{64,112},{80,96},{96,80},{112,64},{1... | collective-permute-start | bytes 184328 | tf_op jit(solution)/shard_map/ppermute | solution.py:698
  63.9 5.7 %collective-permute-start.14 = (f32[120,128]{1,0:T(8,128)S(1)}, f32[120,128]{1,0:T(8,128)S(1)}, u32[]{:S(2)}, u32[]{:S(2)}) collective-permute-start(f32[120,128]{1,0:T(8,128)S(1)} %add.49.refs_0_), channel_id=1, source_target_pairs={{0,64},{16,80},{32,96},{48,112},{64,0},{80,16},{96,32},{112,48},{1... | collective-permute-start | bytes 184328 | tf_op jit(solution)/shard_map/ppermute | solution.py:698
  64.5 6.5 %collective-permute-start.15 = (f32[120,128]{1,0:T(8,128)S(1)}, f32[120,128]{1,0:T(8,128)S(1)}, u32[]{:S(2)}, u32[]{:S(2)}) collective-permute-start(f32[120,128]{1,0:T(8,128)S(1)} %add.49.refs_0_), channel_id=1, source_target_pairs={{0,128},{16,144},{32,160},{48,176},{64,192},{80,208},{96,224},{112... | collective-permute-start | bytes 184328 | tf_op jit(solution)/shard_map/ppermute | solution.py:698
  68.1 5.4 %collective-permute-start.16 = (f32[120,128]{1,0:T(8,128)S(1)}, f32[120,128]{1,0:T(8,128)S(1)}, u32[]{:S(2)}, u32[]{:S(2)}) collective-permute-start(f32[120,128]{1,0:T(8,128)S(1)} %add.49.refs_0_), channel_id=1, source_target_pairs={{0,192},{16,208},{32,224},{48,240},{64,128},{80,144},{96,160},{112... | collective-permute-start | bytes 184328 | tf_op jit(solution)/shard_map/ppermute | solution.py:698
where the time goes:
time: 74.8 us; the launch traced here: 74.4 us
  starting transfers between devices  33.1 us (44%)
  waiting for transfers between devices  18.8 us (25%)
  Pallas kernels  13.1 us (18%)
  local copies, waits for them, and re-layouts  7.61 us (10%)
  between operations  0.9 us (1%)
  other arithmetic  0.86 us (1%)
    ppermute x11, waiting for transfers between devices, shards(): lax.ppermute(mine, axis, [(i, i ^ k) for i in range(count)])  18.8 us
    ppermute x11, starting transfers between devices, shards(): lax.ppermute(mine, axis, [(i, i ^ k) for i in range(count)])  15.4 us
    ppermute x3, starting transfers between devices, swap(): lax.ppermute(second, axis, pairs(1))  13.5 us
    pallas_call x1, Pallas kernels, run_kernel(): pl.pallas_call(unet_tile, out_shape=(jax.ShapeDtypeStruct((2, 128, 256),...  10.8 us
    unnamed x22, local copies, waits for them, and re-layouts  4.75 us
    ppermute x3, starting transfers between devices, swap(): lax.ppermute(first, axis, pairs(0))  4.13 us
  transfers between devices with their start and end apart: 17, of which 10 were waited for; matrix products, arithmetic and copies ran while one was open for 6% of the time, Pallas kernels for 1%

commit v1 on v0

--- a/solution.py
+++ b/solution.py
@@ -56,6 +56,45 @@
 
 def wider(base):
     return lanes([base, jnp.zeros((base.shape[0], 256 - base.shape[1]), F32)])
+
+
+def turned(block):
+    m, n = block.shape
+    if m % 128:
+        block = rows([block, jnp.zeros((128 - m % 128, n), F32)])
+    return block.T
+
+
+def joined_turned(base):
+    block = turned(base)
+    lane = lane_of((8, 128)) >> 3
+    parts = []
+    for f in (1, 0):
+        groups = []
+        for dx in (2, 1, 0):
+            groups.append(sum(
+                roll(
+                    jnp.where(lane == dx, block[64 * dy + 32 * f + 8 * dz : 64 * dy + 32 * f + 8 * dz + 8], 0.0),
+                    32 * (2 - dy) + 8 * (2 - dz) - 8 * dx,
+                )
+                for dy in range(3)
+                for dz in range(3)
+            ))
+        parts.append(lanes(groups + [jnp.zeros((8, 128), F32)]))
+    return rows(parts)
+
+
+def coarse_turned(base):
+    block = turned(base)
+    lane = lane_of((16, 128)) >> 4
+    groups = []
+    for dx in (2, 1, 0):
+        taps = [
+            roll(jnp.where(lane == dx, block[16 * k : 16 * k + 16], 0.0), 16 * ((8 - k) % 8) - 16 * dx)
+            for k in range(9)
+        ]
+        groups.append(lanes([sum(taps[1:]), taps[0]]))
+    return groups
 
 
 def roll(x, shift):
@@ -136,7 +175,7 @@
 
 def kernel(
     pos, wide, beside_0, beside_1, cot,
-    b_first, b_down, b_down_t, b_coarse, b_coarse_t, b_up, b_up_t, b_joined, b_joined_t, wf_col,
+    b_first, b_down, b_coarse, b_up, b_joined, w_last,
     act_own, pay,
     fe, vh, vl, fh, fl, slope_f, pdh, pdl, slope_d, rc, slope_c, ch, cl, pjh, pjl, goh, gol,
     pgh, pgl, gdir, guh, gul, pch, pcl, gch, gcl, rd, gdh, gdl,
@@ -286,7 +325,10 @@
             roll(base[8 * dx : 8 * dx + 8], 64 * b + 8 * c) for dx in range(3) for b in range(2) for c in range(2)
         ])
     )
-    wf_rows = wf_col[...] * scale
+    square = (8, 8)
+    diagonal = lane_of(square) == lax.broadcasted_iota(jnp.int32, square, 0)
+    column = jnp.sum(jnp.where(diagonal, jnp.broadcast_to(w_last[...][:, :8], square), 0.0), axis=1, keepdims=True)
+    wf_rows = rows([column] * 4) * scale
     for x in range(4):
         for ref in (pgh, pgl):
             ref[x, 0:3] = jnp.zeros((3, 32, 128), BF16)
@@ -342,7 +384,7 @@
         for dx in range(3)
     ])
 
-    base = b_joined_t[...]
+    base = joined_turned(b_joined[...])
     w_back = stacked(
         rows([
             roll(base[8 * f : 8 * f + 8], 128 * a + 32 * b + 8 * c)
@@ -352,7 +394,7 @@
             for c in range(2)
         ])
     )
-    w_up_t = stacked(b_up_t[...][:, :64])
+    w_up_t = stacked(turned(b_up[...])[:16, :64])
     for ref in (pch, pcl):
         for at in range(4):
             ref[at, 0:2] = jnp.zeros((2, 48, 128), BF16)
@@ -416,11 +458,8 @@
     to_taps = jnp.where(row_256 == jnp.where(tap < 9, key, -1), 1.0, 0.0).astype(BF16)
     part_joined = by_tap([part_joined[8 * dx : 8 * dx + 8] for dx in range(3)], to_taps)
 
-    base = b_coarse_t[...]
     w_back_coarse = stacked(
-        rows([
-            roll(base[:, 256 * dx : 256 * dx + 256], 48 * k) for dx in range(3) for k in range(2)
-        ])[:, :192]
+        rows([roll(group, 48 * k) for group in coarse_turned(b_coarse[...]) for k in range(2)])[:, :192]
     )
     for pair in range(2):
         for k in range(4):
@@ -449,7 +488,8 @@
         sum(roll(total[256 * a + 32 * y : 256 * a + 32 * y + 32], -16 * y) for y in range(8)) for a in range(2)
     ])
 
-    base = b_down_t[...]
+    base = turned(b_down[...])
+    base = rows([base[0:32], base[128:160]])
     base = thrice(wider(base), 64)
     w_back_down = rows([roll(base[32 * a : 32 * a + 32], 16 * k) for a in range(2) for k in range(4)])
     w_back_down = w_back_down[:, :192].astype(BF16)
@@ -500,14 +540,17 @@
     pay[112:120] = part_first + jnp.where(lane == 64 + row, part_final, 0.0)
 
 
-def image(act_own, wf_lanes, img):
+def image(act_own, w_last, img):
     zt = lane_of((256, 256))
     rt = lax.broadcasted_iota(jnp.int32, (256, 256), 0)
     merge = jnp.where(zt == 2 * (rt & 127) + (rt >> 7), 1.0, 0.0).astype(BF16)
     f_row = lax.broadcasted_iota(jnp.int32, (16, 128), 0)
     f_col = lane_of((16, 128))
+    wf_lanes = w_last[...]
+    for by in (8, 16, 32, 64):
+        wf_lanes = wf_lanes + roll(wf_lanes, by)
     w_final = stacked(
-        jnp.where((f_row >> 3 == (f_col >> 3) & 1) & (f_row & 7 == f_col >> 4), wf_lanes[...], 0.0)
+        jnp.where((f_row >> 3 == (f_col >> 3) & 1) & (f_row & 7 == f_col >> 4), wf_lanes, 0.0)
     )
     out_rows = []
     for at in range(2):
@@ -518,7 +561,7 @@
     img[...] = (whole[:32] + whole[32:]).reshape(4, 8, 256)
 
 
-def run_image(act_own, wf_lanes):
+def run_image(act_own, w_last):
     vmem = pl.BlockSpec(memory_space=pltpu.VMEM)
     return pl.pallas_call(
         image,
@@ -527,7 +570,7 @@
         out_specs=vmem,
         compiler_params=pltpu.CompilerParams(vmem_limit_bytes=8 * 1024 * 1024),
         cost_estimate=pl.CostEstimate(flops=200_000_000, bytes_accessed=400_000, transcendentals=0),
-    )(act_own, wf_lanes)
+    )(act_own, w_last)
 
 
 def exact(block, choice):
@@ -647,24 +690,16 @@
     first = w_first.reshape(3, 3, 3, 8).transpose(3, 0, 2, 1)
     first = padded(first, 8, 4, 4, 16).reshape(8, 256)
     joined = w_joined.reshape(3, 3, 3, 8, 2, 8)
-    joined_out = padded(joined.transpose(0, 3, 1, 4, 2, 5), 3, 8, 4, 2, 4, 8).reshape(24, 256)
-    joined_t = joined[::-1, ::-1, ::-1, :, ::-1].transpose(4, 5, 0, 1, 2, 3)
-    joined_t = padded(joined_t, 2, 8, 4, 4, 4, 8).reshape(16, 512)
-    wf_lanes = jnp.tile(w_final, (1, 16))
-    wf_col = jnp.tile(w_final.reshape(8, 1), (4, 1))
-    return first, joined_out, joined_t, wf_lanes, wf_col
+    joined = padded(joined.transpose(0, 3, 1, 4, 2, 5), 3, 8, 4, 2, 4, 8).reshape(24, 256)
+    return first, joined, padded(w_final, 1, 128)
 
 
 def bases_later(w_down, w_coarse, w_up):
     down = padded(w_down.transpose(0, 2, 3, 4, 1).reshape(16, 2, 32), 16, 2, 128).reshape(16, 256)
-    down_t = padded(w_down.transpose(2, 3, 4, 1, 0).reshape(64, 16), 64, 128)
     coarse = w_coarse.reshape(3, 3, 3, 16, 16)
-    coarse_out = padded(coarse.transpose(0, 3, 1, 2, 4).reshape(48, 144), 48, 256)
-    coarse_t = coarse[::-1, ::-1, ::-1].transpose(4, 0, 1, 2, 3).reshape(16, 3, 144)
-    coarse_t = padded(coarse_t, 16, 3, 256).reshape(16, 768)
+    coarse = padded(coarse.transpose(0, 3, 1, 2, 4).reshape(48, 144), 48, 256)
     up = padded(w_up.transpose(2, 3, 4, 0, 1).reshape(64, 16), 64, 128)
-    up_t = padded(w_up.transpose(1, 2, 3, 4, 0).reshape(16, 64), 16, 128)
-    return down, down_t, coarse_out, coarse_t, up, up_t
+    return down, coarse, up
 
 
 def shards(in_field, cotangent, w_first, w_down, w_coarse, w_up, w_joined, w_final):
@@ -681,9 +716,9 @@
     )
     wide, *sent = run_strips([pos, field, *near, *far])
     beside = swap(*sent, "gy", 1)
-    first, joined_out, joined_t, wf_lanes, wf_col = now
+    first, joined, last = now
     later = bases_later(w_down, w_coarse, w_up)
-    weights = [first, *later, joined_out, joined_t, wf_col]
+    weights = [first, *later, joined, last]
 
     scale = 1.0 / math.sqrt(size_x * size_y * in_field.shape[3])
     act_own, pay = run_kernel([pos, wide, *beside, cot, *weights], scale, size_x, size_y)
@@ -698,7 +733,7 @@
             blocks = [mine] + [lax.ppermute(mine, axis, [(i, i ^ k) for i in range(count)]) for k in partners]
             if imitated is None:
                 act_own, blocks = lax.optimization_barrier((act_own, blocks))
-                imitated = run_image(act_own, wf_lanes)
+                imitated = run_image(act_own, last)
     coarse, joined, first, down, up, final = run_outputs(blocks)
     return (
         imitated[None],

time: 74.8 us -> 73.6 us (0.984)
  local copies, waits for them, and re-layouts: 7.61 us -> 5.09 us
  starting transfers between devices: 33.1 us -> 35.4 us
  waiting for transfers between devices: 18.8 us -> 17.6 us
    ppermute x11, starting transfers between devices: 15.4 us -> 17.7 us  [shards(): lax.ppermute(mine, axis, [(i, i ^ k) for i in range(count)])]
    ppermute x11, waiting for transfers between devices: 18.8 us -> 16.8 us  [shards(): lax.ppermute(mine, axis, [(i, i ^ k) for i in range(count)])]
    unnamed x22 -> x18, local copies, waits for them, and re-layouts: 4.75 us -> 3.76 us
  transfers between devices with their start and end apart: 17 -> 17, of which waited for: 10 -> 11; matrix products, arithmetic and copies ran while one was open for 6% -> 5% of each run, Pallas kernels for 1% -> 2%
where the time goes in v1:
time: 73.6 us; the launch traced here: 73.2 us
  starting transfers between devices  35.4 us (48%)
  waiting for transfers between devices  17.6 us (24%)
  Pallas kernels  13.5 us (18%)
  local copies, waits for them, and re-layouts  5.09 us (7%)
  other arithmetic  0.86 us (1%)
  between operations  0.81 us (1%)
    ppermute x11, starting transfers between devices, shards(): lax.ppermute(mine, axis, [(i, i ^ k) for i in range(count)])  17.7 us
    ppermute x11, waiting for transfers between devices, shards(): lax.ppermute(mine, axis, [(i, i ^ k) for i in range(count)])  16.8 us
    ppermute x3, starting transfers between devices, swap(): lax.ppermute(second, axis, pairs(1))  13.5 us
    pallas_call x1, Pallas kernels, run_kernel(): pl.pallas_call(unet_tile, out_shape=(jax.ShapeDtypeStruct((2, 128, 256),...  10.9 us
    ppermute x3, starting transfers between devices, swap(): lax.ppermute(first, axis, pairs(0))  4.13 us
    unnamed x18, local copies, waits for them, and re-layouts  3.76 us
  transfers between devices with their start and end apart: 17, of which 11 were waited for; matrix products, arithmetic and copies ran while one was open for 5% of the time, Pallas kernels for 2%

profile of v1, /device:TPU:6, one launch (start us, length us, event | category | flops | bytes accessed | tf_op | source)
XLA Modules:
  0.0 73.2 jit_solution(11839625340731920447)
XLA Ops:
  0.6 3.4 %collective-permute-start = (f32[4,8,256]{2,1,0:T(8,128)}, f32[4,8,256]{2,1,0:T(8,128)S(1)}, u32[]{:S(2)}, u32[]{:S(2)}) collective-permute-start(f32[4,8,256]{2,1,0:T(8,128)} %bitcast.30), channel_id=1, source_target_pairs={{0,16},{16,0},{32,48},{48,32},{64,80},{80,64},{96,112},{112,96},{1... | collective-permute-start | bytes 98312 | tf_op jit(solution)/shard_map/ppermute | solution.py:675
  4.0 4.7 %collective-permute-start.1 = (f32[4,8,256]{2,1,0:T(8,128)}, f32[4,8,256]{2,1,0:T(8,128)S(1)}, u32[]{:S(2)}, u32[]{:S(2)}) collective-permute-start(f32[4,8,256]{2,1,0:T(8,128)} %bitcast.31), channel_id=1, source_target_pairs={{0,240},{16,32},{32,16},{48,64},{64,48},{80,96},{96,80},{112,128},... | collective-permute-start | bytes 98312 | tf_op jit(solution)/shard_map/ppermute | solution.py:675
  8.7 0.7 %select_bitcast_fusion = (f32[1,8,256]{2,1,0:T(8,128)S(1)}, f32[1,8,256]{2,1,0:T(8,128)S(1)}) fusion(f32[1,4,8,256]{3,2,1,0:T(8,128)} %param.8, pred[]{:T(512)S(6)} %eq.3), kind=kLoop, calls=%fused_computation.2 | loop fusion | flops 4096 | bytes 32769 | tf_op jit(solution)/shard_map/jit(_where)/select_n | solution.py:712
  9.5 0.7 collective-permute-start.2
  10.2 5.2 %collective-permute-start.3 = (f32[1,8,256]{2,1,0:T(8,128)S(1)}, f32[1,8,256]{2,1,0:T(8,128)S(1)}, u32[]{:S(2)}, u32[]{:S(2)}) collective-permute-start(f32[1,8,256]{2,1,0:T(8,128)S(1)} %get-tuple-element.61), channel_id=1, source_target_pairs={{0,224},{16,240},{32,64},{48,80},{64,32},{80,48},{96,128},{112,144... | collective-permute-start | bytes 24584 | tf_op jit(solution)/shard_map/ppermute | solution.py:675
  15.4 0.1 pad_add_fusion.pos.refs_0_
  15.5 1.0 %copy.21 = f32[27,8,16]{2,1,0:T(8,128)S(1)} copy(f32[27,8,16]{0,2,1:T(8,128)} %param.14) | data formatting | bytes 27648 | tf_op args[6]
  16.4 0.2 reshape.95
  16.6 0.1 copy.30
  16.7 0.1 pad.25.clone
  16.8 0.0 copy-start.5
  16.8 0.4 reshape.96.refs_9_
  17.2 0.3 copy-done.5
  17.5 0.1 copy.19
  17.6 0.2 copy.29
  17.8 0.0 copy-start.2
  17.8 0.0 copy-start.6
  17.8 0.0 copy-start
  17.8 0.1 reshape.94.refs_5_
  17.9 0.6 copy-done.6
  18.5 0.0 collective-permute-done.2.far_0
  18.5 0.1 collective-permute-done.3.far_1
  18.6 0.0 collective-permute-done.near_0
  18.6 0.0 collective-permute-done.1.near_1
  18.6 0.0 copy-done
  18.6 0.6 shard_map.135
  19.2 0.1 collective-permute-start.4
  19.3 3.6 %collective-permute-start.5 = (f32[70,256]{1,0:T(8,128)S(1)}, f32[70,256]{1,0:T(8,128)S(1)}, u32[]{:S(2)}, u32[]{:S(2)}) collective-permute-start(f32[70,256]{1,0:T(8,128)S(1)} %get-tuple-element.41), channel_id=1, source_target_pairs={{0,15},{1,2},{2,1},{3,4},{4,3},{5,6},{6,5},{7,8},{8,7},{9,10},{10,... | collective-permute-start | bytes 215048 | tf_op jit(solution)/shard_map/ppermute | solution.py:675
  22.9 0.0 copy-done.2
  22.9 0.2 copy.25
  23.1 0.1 copy.26
  23.2 0.2 reshape.100
  23.4 0.7 %copy-done.3 = f32[16,8,2,2,2]{0,4,3,2,1:T(2,128)S(1)} copy-done((f32[16,8,2,2,2]{0,4,3,2,1:T(2,128)S(1)}, f32[16,8,2,2,2]{0,4,3,2,1:T(2,128)}, u32[]{:S(2)}) %copy-start.3) | copy-done | bytes 4120
  24.1 0.0 copy-start.4
  24.1 0.1 copy.28.refs_6_
  24.2 0.7 copy-done.4
  24.9 0.0 collective-permute-done.4.refs_2_
  24.9 0.6 collective-permute-done.5.refs_3_
  25.5 0.1 copy-done.1
  25.7 10.9 %shard_map.136 = (f32[2,128,256]{2,1,0:T(8,128)S(1)}, f32[120,128]{1,0:T(8,128)S(1)}) custom-call(s32[2]{0:T(128)S(1)} %pad_add_fusion.pos.refs_0_, f32[14,8,256]{2,1,0:T(8,128)S(1)} %get-tuple-element.39.refs_1_, f32[70,256]{1,0:T(8,128)S(1)} %collective-permute-done.4.refs_2_, f32[70,256]{1,0:T(8,128)S(1)} %collective-permute-done.5.refs_3_, ...), custom_call_target="tpu_custom_call" | custom-call | flops 3000000000 | bytes 2000000 | tf_op jit(solution)/shard_map/pallas_call | solution.py:658
  36.6 0.1 collective-permute-start.6
  36.7 0.3 collective-permute-start.7
  37.0 1.5 %collective-permute-start.8 = (f32[120,128]{1,0:T(8,128)S(1)}, f32[120,128]{1,0:T(8,128)S(1)}, u32[]{:S(2)}, u32[]{:S(2)}) collective-permute-start(f32[120,128]{1,0:T(8,128)S(1)} %get-tuple-element.51), channel_id=1, source_target_pairs={{0,3},{1,2},{2,1},{3,0},{4,7},{5,6},{6,5},{7,4},{8,11},{9,10},{10,... | collective-permute-start | bytes 184328 | tf_op jit(solution)/shard_map/ppermute | solution.py:733
  38.6 0.0 collective-permute-done.6
  38.6 3.0 %collective-permute-done.7 = f32[120,128]{1,0:T(8,128)S(1)} collective-permute-done((f32[120,128]{1,0:T(8,128)S(1)}, f32[120,128]{1,0:T(8,128)S(1)}, u32[]{:S(2)}, u32[]{:S(2)}) %collective-permute-start.7) | collective-permute-done | bytes 61472 | tf_op jit(solution)/shard_map/ppermute | solution.py:733
  41.6 0.4 collective-permute-done.8
  42.0 2.3 %collective-permute-start.10 = (f32[120,128]{1,0:T(8,128)S(1)}, f32[120,128]{1,0:T(8,128)S(1)}, u32[]{:S(2)}, u32[]{:S(2)}) collective-permute-start(f32[120,128]{1,0:T(8,128)S(1)} %add_add_fusion.1), channel_id=1, source_target_pairs={{0,8},{1,9},{2,10},{3,11},{4,12},{5,13},{6,14},{7,15},{8,0},{9,1},... | collective-permute-start | bytes 184328 | tf_op jit(solution)/shard_map/ppermute | solution.py:733
  44.3 1.4 %collective-permute-start.11 = (f32[120,128]{1,0:T(8,128)S(1)}, f32[120,128]{1,0:T(8,128)S(1)}, u32[]{:S(2)}, u32[]{:S(2)}) collective-permute-start(f32[120,128]{1,0:T(8,128)S(1)} %add_add_fusion.1), channel_id=1, source_target_pairs={{0,12},{1,13},{2,14},{3,15},{4,8},{5,9},{6,10},{7,11},{8,4},{9,5},... | collective-permute-start | bytes 184328 | tf_op jit(solution)/shard_map/ppermute | solution.py:733
  45.7 0.3 collective-permute-start.9
  46.0 1.8 %collective-permute-done.10 = f32[120,128]{1,0:T(8,128)S(1)} collective-permute-done((f32[120,128]{1,0:T(8,128)S(1)}, f32[120,128]{1,0:T(8,128)S(1)}, u32[]{:S(2)}, u32[]{:S(2)}) %collective-permute-start.10) | collective-permute-done | bytes 61472 | tf_op jit(solution)/shard_map/ppermute | solution.py:733
  47.8 1.9 %collective-permute-done.11 = f32[120,128]{1,0:T(8,128)S(1)} collective-permute-done((f32[120,128]{1,0:T(8,128)S(1)}, f32[120,128]{1,0:T(8,128)S(1)}, u32[]{:S(2)}, u32[]{:S(2)}) %collective-permute-start.11) | collective-permute-done | bytes 61472 | tf_op jit(solution)/shard_map/ppermute | solution.py:733
  49.7 0.2 collective-permute-done.9
  49.9 2.2 %collective-permute-start.12 = (f32[120,128]{1,0:T(8,128)S(1)}, f32[120,128]{1,0:T(8,128)S(1)}, u32[]{:S(2)}, u32[]{:S(2)}) collective-permute-start(f32[120,128]{1,0:T(8,128)S(1)} %add_add_fusion), channel_id=1, source_target_pairs={{0,16},{16,0},{32,48},{48,32},{64,80},{80,64},{96,112},{112,96},{1... | collective-permute-start | bytes 184328 | tf_op jit(solution)/shard_map/ppermute | solution.py:733
  52.1 3.9 %collective-permute-done.12 = f32[120,128]{1,0:T(8,128)S(1)} collective-permute-done((f32[120,128]{1,0:T(8,128)S(1)}, f32[120,128]{1,0:T(8,128)S(1)}, u32[]{:S(2)}, u32[]{:S(2)}) %collective-permute-start.12) | collective-permute-done | bytes 61472 | tf_op jit(solution)/shard_map/ppermute | solution.py:733
  56.0 4.7 %collective-permute-start.13 = (f32[120,128]{1,0:T(8,128)S(1)}, f32[120,128]{1,0:T(8,128)S(1)}, u32[]{:S(2)}, u32[]{:S(2)}) collective-permute-start(f32[120,128]{1,0:T(8,128)S(1)} %add.42), channel_id=1, source_target_pairs={{0,48},{16,32},{32,16},{48,0},{64,112},{80,96},{96,80},{112,64},{1... | collective-permute-start | bytes 184328 | tf_op jit(solution)/shard_map/ppermute | solution.py:733
  60.8 2.4 %collective-permute-done.13 = f32[120,128]{1,0:T(8,128)S(1)} collective-permute-done((f32[120,128]{1,0:T(8,128)S(1)}, f32[120,128]{1,0:T(8,128)S(1)}, u32[]{:S(2)}, u32[]{:S(2)}) %collective-permute-start.13) | collective-permute-done | bytes 61472 | tf_op jit(solution)/shard_map/ppermute | solution.py:733
  63.2 0.2 collective-permute-start.14
  63.4 3.6 %collective-permute-start.15 = (f32[120,128]{1,0:T(8,128)S(1)}, f32[120,128]{1,0:T(8,128)S(1)}, u32[]{:S(2)}, u32[]{:S(2)}) collective-permute-start(f32[120,128]{1,0:T(8,128)S(1)} %add.43.refs_0_), channel_id=1, source_target_pairs={{0,128},{16,144},{32,160},{48,176},{64,192},{80,208},{96,224},{112... | collective-permute-start | bytes 184328 | tf_op jit(solution)/shard_map/ppermute | solution.py:733
  67.0 1.0 %collective-permute-start.16 = (f32[120,128]{1,0:T(8,128)S(1)}, f32[120,128]{1,0:T(8,128)S(1)}, u32[]{:S(2)}, u32[]{:S(2)}) collective-permute-start(f32[120,128]{1,0:T(8,128)S(1)} %add.43.refs_0_), channel_id=1, source_target_pairs={{0,192},{16,208},{32,224},{48,240},{64,128},{80,144},{96,160},{112... | collective-permute-start | bytes 184328 | tf_op jit(solution)/shard_map/ppermute | solution.py:733
  68.0 1.2 %shard_map.137 = f32[4,8,256]{2,1,0:T(8,128)} custom-call(f32[2,128,256]{2,1,0:T(8,128)S(1)} %get-tuple-element.50.act_own, f32[1,128]{1,0:T(1,128)S(1)} %pad.26.refs_10_.w_last), custom_call_target="tpu_custom_call" | custom-call | flops 200000000 | bytes 400000 | tf_op jit(solution)/shard_map/pallas_call | solution.py:566
  69.2 0.0 collective-permute-done.14.refs_1_
  69.2 0.6 collective-permute-done.15.refs_2_
  69.8 2.6 %collective-permute-done.16.refs_3_ = f32[120,128]{1,0:T(8,128)S(1)} collective-permute-done((f32[120,128]{1,0:T(8,128)S(1)}, f32[120,128]{1,0:T(8,128)S(1)}, u32[]{:S(2)}, u32[]{:S(2)}) %collective-permute-start.16) | collective-permute-done | bytes 61472 | tf_op jit(solution)/shard_map/ppermute | solution.py:733
  72.4 0.8 %shard_map.138 = (f32[16,16,27]{2,1,0:T(8,128)}, f32[8,16,27]{2,1,0:T(8,128)}, f32[8,1,27]{2,1,0:T(1,128)}, f32[8,4,2,16]{3,2,1,0:T(2,128)}, f32[8,4,2,16]{3,2,1,0:T(2,128)}, /*index=5*/f32[1,8]{1,0:T(1,128)}) custom-call(f32[120,128]{1,0:T(8,128)S(1)} %add.43.refs_0_, f32[120,128]{1,0:T(8,128)S(1)} %collective-permute-done.14.refs_1_, ...), custom_call_target="tpu_custom_call" | custom-call | tf_op jit(solution)/shard_map/pallas_call | solution.py:616
  (14 shorter events, 0.1 us)
Async XLA Ops:
  0.6 18.0 %collective-permute-start = (f32[4,8,256]{2,1,0:T(8,128)}, f32[4,8,256]{2,1,0:T(8,128)S(1)}, u32[]{:S(2)}, u32[]{:S(2)}) collective-permute-start(f32[4,8,256]{2,1,0:T(8,128)} %bitcast.30), channel_id=1, source_target_pairs={{0,16},{16,0},{32,48},{48,32},{64,80},{80,64},{96,112},{112,96},{1... | collective-permute-start | bytes 98312 | tf_op jit(solution)/shard_map/ppermute | solution.py:675
  4.0 14.6 %collective-permute-start.1 = (f32[4,8,256]{2,1,0:T(8,128)}, f32[4,8,256]{2,1,0:T(8,128)S(1)}, u32[]{:S(2)}, u32[]{:S(2)}) collective-permute-start(f32[4,8,256]{2,1,0:T(8,128)} %bitcast.31), channel_id=1, source_target_pairs={{0,240},{16,32},{32,16},{48,64},{64,48},{80,96},{96,80},{112,128},... | collective-permute-start | bytes 98312 | tf_op jit(solution)/shard_map/ppermute | solution.py:675
  9.5 9.0 %collective-permute-start.2 = (f32[1,8,256]{2,1,0:T(8,128)S(1)}, f32[1,8,256]{2,1,0:T(8,128)S(1)}, u32[]{:S(2)}, u32[]{:S(2)}) collective-permute-start(f32[1,8,256]{2,1,0:T(8,128)S(1)} %get-tuple-element.62), channel_id=1, source_target_pairs={{0,32},{16,48},{32,0},{48,16},{64,96},{80,112},{96,64},{112,80},{1... | collective-permute-start | bytes 24584 | tf_op jit(solution)/shard_map/ppermute | solution.py:675
  10.2 8.5 %collective-permute-start.3 = (f32[1,8,256]{2,1,0:T(8,128)S(1)}, f32[1,8,256]{2,1,0:T(8,128)S(1)}, u32[]{:S(2)}, u32[]{:S(2)}) collective-permute-start(f32[1,8,256]{2,1,0:T(8,128)S(1)} %get-tuple-element.61), channel_id=1, source_target_pairs={{0,224},{16,240},{32,64},{48,80},{64,32},{80,48},{96,128},{112,144... | collective-permute-start | bytes 24584 | tf_op jit(solution)/shard_map/ppermute | solution.py:675
  16.8 0.7 copy-start.5
  17.8 5.1 %copy-start.2 = (f32[27,16,16]{0,2,1:T(8,128)S(1)}, f32[27,16,16]{0,2,1:T(8,128)}, u32[]{:S(2)}) copy-start(f32[27,16,16]{0,2,1:T(8,128)} %param.12) | copy-start | bytes 82948
  17.8 0.7 copy-start.6
  17.8 0.8 %copy-start = (f32[1,4,8,256]{3,2,1,0:T(8,128)S(1)}, f32[1,4,8,256]{3,2,1,0:T(8,128)}, u32[]{:S(2)}) copy-start(f32[1,4,8,256]{3,2,1,0:T(8,128)} %param.8) | copy-start | bytes 98308
  19.2 5.7 %collective-permute-start.4 = (f32[70,256]{1,0:T(8,128)S(1)}, f32[70,256]{1,0:T(8,128)S(1)}, u32[]{:S(2)}, u32[]{:S(2)}) collective-permute-start(f32[70,256]{1,0:T(8,128)S(1)} %get-tuple-element.40), channel_id=1, source_target_pairs={{0,1},{1,0},{2,3},{3,2},{4,5},{5,4},{6,7},{7,6},{8,9},{9,8},{10,11... | collective-permute-start | bytes 215048 | tf_op jit(solution)/shard_map/ppermute | solution.py:675
  19.3 6.2 %collective-permute-start.5 = (f32[70,256]{1,0:T(8,128)S(1)}, f32[70,256]{1,0:T(8,128)S(1)}, u32[]{:S(2)}, u32[]{:S(2)}) collective-permute-start(f32[70,256]{1,0:T(8,128)S(1)} %get-tuple-element.41), channel_id=1, source_target_pairs={{0,15},{1,2},{2,1},{3,4},{4,3},{5,6},{6,5},{7,8},{8,7},{9,10},{10,... | collective-permute-start | bytes 215048 | tf_op jit(solution)/shard_map/ppermute | solution.py:675
  23.3 0.8 %copy-start.3 = (f32[16,8,2,2,2]{0,4,3,2,1:T(2,128)S(1)}, f32[16,8,2,2,2]{0,4,3,2,1:T(2,128)}, u32[]{:S(2)}) copy-start(f32[16,8,2,2,2]{0,4,3,2,1:T(2,128)} %param.11) | copy-start | bytes 12292
  24.1 0.8 %copy-start.4 = (f32[8,16,2,2,2]{1,4,3,2,0:T(2,128)S(1)}, f32[8,16,2,2,2]{1,4,3,2,0:T(2,128)}, u32[]{:S(2)}) copy-start(f32[8,16,2,2,2]{1,4,3,2,0:T(2,128)} %param.13) | copy-start | bytes 12292
  24.9 0.8 %copy-start.1 = (f32[1,4,8,256]{3,2,1,0:T(8,128)S(1)}, f32[1,4,8,256]{3,2,1,0:T(8,128)}, u32[]{:S(2)}) copy-start(f32[1,4,8,256]{3,2,1,0:T(8,128)} %param.9) | copy-start | bytes 98308
  36.6 2.0 %collective-permute-start.6 = (f32[120,128]{1,0:T(8,128)S(1)}, f32[120,128]{1,0:T(8,128)S(1)}, u32[]{:S(2)}, u32[]{:S(2)}) collective-permute-start(f32[120,128]{1,0:T(8,128)S(1)} %get-tuple-element.51), channel_id=1, source_target_pairs={{0,1},{1,0},{2,3},{3,2},{4,5},{5,4},{6,7},{7,6},{8,9},{9,8},{10,11... | collective-permute-start | bytes 184328 | tf_op jit(solution)/shard_map/ppermute | solution.py:733
  36.7 4.9 %collective-permute-start.7 = (f32[120,128]{1,0:T(8,128)S(1)}, f32[120,128]{1,0:T(8,128)S(1)}, u32[]{:S(2)}, u32[]{:S(2)}) collective-permute-start(f32[120,128]{1,0:T(8,128)S(1)} %get-tuple-element.51), channel_id=1, source_target_pairs={{0,2},{1,3},{2,0},{3,1},{4,6},{5,7},{6,4},{7,5},{8,10},{9,11},{10,... | collective-permute-start | bytes 184328 | tf_op jit(solution)/shard_map/ppermute | solution.py:733
  37.0 4.9 %collective-permute-start.8 = (f32[120,128]{1,0:T(8,128)S(1)}, f32[120,128]{1,0:T(8,128)S(1)}, u32[]{:S(2)}, u32[]{:S(2)}) collective-permute-start(f32[120,128]{1,0:T(8,128)S(1)} %get-tuple-element.51), channel_id=1, source_target_pairs={{0,3},{1,2},{2,1},{3,0},{4,7},{5,6},{6,5},{7,4},{8,11},{9,10},{10,... | collective-permute-start | bytes 184328 | tf_op jit(solution)/shard_map/ppermute | solution.py:733
  42.0 5.8 %collective-permute-start.10 = (f32[120,128]{1,0:T(8,128)S(1)}, f32[120,128]{1,0:T(8,128)S(1)}, u32[]{:S(2)}, u32[]{:S(2)}) collective-permute-start(f32[120,128]{1,0:T(8,128)S(1)} %add_add_fusion.1), channel_id=1, source_target_pairs={{0,8},{1,9},{2,10},{3,11},{4,12},{5,13},{6,14},{7,15},{8,0},{9,1},... | collective-permute-start | bytes 184328 | tf_op jit(solution)/shard_map/ppermute | solution.py:733
  44.3 5.4 %collective-permute-start.11 = (f32[120,128]{1,0:T(8,128)S(1)}, f32[120,128]{1,0:T(8,128)S(1)}, u32[]{:S(2)}, u32[]{:S(2)}) collective-permute-start(f32[120,128]{1,0:T(8,128)S(1)} %add_add_fusion.1), channel_id=1, source_target_pairs={{0,12},{1,13},{2,14},{3,15},{4,8},{5,9},{6,10},{7,11},{8,4},{9,5},... | collective-permute-start | bytes 184328 | tf_op jit(solution)/shard_map/ppermute | solution.py:733
  45.7 4.2 %collective-permute-start.9 = (f32[120,128]{1,0:T(8,128)S(1)}, f32[120,128]{1,0:T(8,128)S(1)}, u32[]{:S(2)}, u32[]{:S(2)}) collective-permute-start(f32[120,128]{1,0:T(8,128)S(1)} %add_add_fusion.1), channel_id=1, source_target_pairs={{0,4},{1,5},{2,6},{3,7},{4,0},{5,1},{6,2},{7,3},{8,12},{9,13},{10,... | collective-permute-start | bytes 184328 | tf_op jit(solution)/shard_map/ppermute | solution.py:733
  49.9 6.1 %collective-permute-start.12 = (f32[120,128]{1,0:T(8,128)S(1)}, f32[120,128]{1,0:T(8,128)S(1)}, u32[]{:S(2)}, u32[]{:S(2)}) collective-permute-start(f32[120,128]{1,0:T(8,128)S(1)} %add_add_fusion), channel_id=1, source_target_pairs={{0,16},{16,0},{32,48},{48,32},{64,80},{80,64},{96,112},{112,96},{1... | collective-permute-start | bytes 184328 | tf_op jit(solution)/shard_map/ppermute | solution.py:733
  56.0 7.2 %collective-permute-start.13 = (f32[120,128]{1,0:T(8,128)S(1)}, f32[120,128]{1,0:T(8,128)S(1)}, u32[]{:S(2)}, u32[]{:S(2)}) collective-permute-start(f32[120,128]{1,0:T(8,128)S(1)} %add.42), channel_id=1, source_target_pairs={{0,48},{16,32},{32,16},{48,0},{64,112},{80,96},{96,80},{112,64},{1... | collective-permute-start | bytes 184328 | tf_op jit(solution)/shard_map/ppermute | solution.py:733
  63.2 6.0 %collective-permute-start.14 = (f32[120,128]{1,0:T(8,128)S(1)}, f32[120,128]{1,0:T(8,128)S(1)}, u32[]{:S(2)}, u32[]{:S(2)}) collective-permute-start(f32[120,128]{1,0:T(8,128)S(1)} %add.43.refs_0_), channel_id=1, source_target_pairs={{0,64},{16,80},{32,96},{48,112},{64,0},{80,16},{96,32},{112,48},{1... | collective-permute-start | bytes 184328 | tf_op jit(solution)/shard_map/ppermute | solution.py:733
  63.4 6.4 %collective-permute-start.15 = (f32[120,128]{1,0:T(8,128)S(1)}, f32[120,128]{1,0:T(8,128)S(1)}, u32[]{:S(2)}, u32[]{:S(2)}) collective-permute-start(f32[120,128]{1,0:T(8,128)S(1)} %add.43.refs_0_), channel_id=1, source_target_pairs={{0,128},{16,144},{32,160},{48,176},{64,192},{80,208},{96,224},{112... | collective-permute-start | bytes 184328 | tf_op jit(solution)/shard_map/ppermute | solution.py:733
  67.0 5.4 %collective-permute-start.16 = (f32[120,128]{1,0:T(8,128)S(1)}, f32[120,128]{1,0:T(8,128)S(1)}, u32[]{:S(2)}, u32[]{:S(2)}) collective-permute-start(f32[120,128]{1,0:T(8,128)S(1)} %add.43.refs_0_), channel_id=1, source_target_pairs={{0,192},{16,208},{32,224},{48,240},{64,128},{80,144},{96,160},{112... | collective-permute-start | bytes 184328 | tf_op jit(solution)/shard_map/ppermute | solution.py:733

commit v2 on v1

--- a/solution.py
+++ b/solution.py
@@ -493,7 +493,7 @@
     base = thrice(wider(base), 64)
     w_back_down = rows([roll(base[32 * a : 32 * a + 32], 16 * k) for a in range(2) for k in range(4)])
     w_back_down = w_back_down[:, :192].astype(BF16)
-    total = jnp.zeros((128, 256), F32)
+    total = jnp.zeros((128, 192), F32)
     for pair in range(3):
         for window in range(2):
             mine = slice(64 * window, 64 * window + 64)
@@ -513,10 +513,8 @@
                         half = half + rows(blocks)
                     halves.append(half)
                 high, low = split(lanes(halves) * slope_f[at, 128 * window : 128 * window + 128])
-                pad = jnp.zeros((64, 256), BF16)
-                total = total + nt3(
-                    high, low, rows([first_rhs(vh, at, window), pad]), rows([first_rhs(vl, at, window), pad])
-                )
+                total = total + nt3(high, low, first_rhs(vh, at, window), first_rhs(vl, at, window))
+    total = lanes([total, jnp.zeros((128, 64), F32)])
     part_first = sum(
         roll(total[16 * y + 8 * c : 16 * y + 8 * c + 8], -(y + 16 * c)) for y in range(8) for c in range(2)
     )
@@ -709,8 +707,10 @@
     pos = jnp.stack([lax.axis_index("gx"), lax.axis_index("gy")]).astype(jnp.int32)
     even = ((lax.axis_index("gx") >> 1) & 1) == 0
     low, high = field[:1], field[3:]
-    far = swap(jnp.where(even, high, low), jnp.where(even, low, high), "gx", 2)
-    near = swap(field, field, "gx", 1)
+    low, high = jnp.where(even, high, low), jnp.where(even, low, high)
+    low, high, tile = lax.optimization_barrier((low, high, field))
+    near = swap(tile, tile, "gx", 1)
+    far = swap(low, high, "gx", 2)
     near, far, now, pos, (w_down, w_coarse, w_up) = lax.optimization_barrier(
         (near, far, now, pos, (w_down, w_coarse, w_up))
     )

time: 73.6 us -> 73.6 us (level)
  transfers between devices with their start and end apart: 17 -> 17, of which waited for: 11 -> 11; matrix products, arithmetic and copies ran while one was open for 5% -> 4% of each run, Pallas kernels for 2% -> 2%
where the time goes in v2:
time: 73.6 us; the launch traced here: 73.2 us
  starting transfers between devices  35.4 us (48%)
  waiting for transfers between devices  17.5 us (24%)
  Pallas kernels  13.5 us (18%)
  local copies, waits for them, and re-layouts  5.1 us (7%)
  other arithmetic  0.88 us (1%)
  between operations  0.81 us (1%)
    ppermute x11, starting transfers between devices, shards(): lax.ppermute(mine, axis, [(i, i ^ k) for i in range(count)])  17.8 us
    ppermute x11, waiting for transfers between devices, shards(): lax.ppermute(mine, axis, [(i, i ^ k) for i in range(count)])  16.8 us
    ppermute x3, starting transfers between devices, swap(): lax.ppermute(second, axis, pairs(1))  13.6 us
    pallas_call x1, Pallas kernels, run_kernel(): pl.pallas_call(unet_tile, out_shape=(jax.ShapeDtypeStruct((2, 128, 256),...  10.9 us
    ppermute x3, starting transfers between devices, swap(): lax.ppermute(first, axis, pairs(0))  4.01 us
    unnamed x18, local copies, waits for them, and re-layouts  3.77 us
  transfers between devices with their start and end apart: 17, of which 11 were waited for; matrix products, arithmetic and copies ran while one was open for 4% of the time, Pallas kernels for 2%

profile of v2, /device:TPU:6, one launch (start us, length us, event | category | flops | bytes accessed | tf_op | source)
XLA Modules:
  0.0 73.2 jit_solution(2648315380220245604)
XLA Ops:
  0.6 0.0 copy-start
  0.7 0.8 %select_bitcast_fusion = (f32[1,8,256]{2,1,0:T(8,128)S(1)}, f32[1,8,256]{2,1,0:T(8,128)S(1)}) fusion(f32[1,4,8,256]{3,2,1,0:T(8,128)} %param.8, pred[]{:T(512)S(6)} %eq.3), kind=kLoop, calls=%fused_computation.2 | loop fusion | flops 4096 | bytes 32769 | tf_op jit(solution)/shard_map/jit(_where)/select_n | solution.py:710
  1.4 0.0 copy-done
  1.4 3.3 %collective-permute-start = (f32[4,8,256]{2,1,0:T(8,128)S(1)}, f32[4,8,256]{2,1,0:T(8,128)S(1)}, u32[]{:S(2)}, u32[]{:S(2)}) collective-permute-start(f32[4,8,256]{2,1,0:T(8,128)S(1)} %bitcast.30), channel_id=1, source_target_pairs={{0,16},{16,0},{32,48},{48,32},{64,80},{80,64},{96,112},{112,96},{1... | collective-permute-start | bytes 98312 | tf_op jit(solution)/shard_map/ppermute | solution.py:673
  4.7 4.7 %collective-permute-start.1 = (f32[4,8,256]{2,1,0:T(8,128)S(1)}, f32[4,8,256]{2,1,0:T(8,128)S(1)}, u32[]{:S(2)}, u32[]{:S(2)}) collective-permute-start(f32[4,8,256]{2,1,0:T(8,128)S(1)} %bitcast.31), channel_id=1, source_target_pairs={{0,240},{16,32},{32,16},{48,64},{64,48},{80,96},{96,80},{112,128},... | collective-permute-start | bytes 98312 | tf_op jit(solution)/shard_map/ppermute | solution.py:673
  9.4 0.6 collective-permute-start.2
  10.1 5.3 %collective-permute-start.3 = (f32[1,8,256]{2,1,0:T(8,128)S(1)}, f32[1,8,256]{2,1,0:T(8,128)S(1)}, u32[]{:S(2)}, u32[]{:S(2)}) collective-permute-start(f32[1,8,256]{2,1,0:T(8,128)S(1)} %get-tuple-element.39), channel_id=1, source_target_pairs={{0,224},{16,240},{32,64},{48,80},{64,32},{80,48},{96,128},{112,144... | collective-permute-start | bytes 24584 | tf_op jit(solution)/shard_map/ppermute | solution.py:673
  15.3 0.1 pad_add_fusion.pos.refs_0_
  15.4 1.0 %copy.21 = f32[27,8,16]{2,1,0:T(8,128)S(1)} copy(f32[27,8,16]{0,2,1:T(8,128)} %param.14) | data formatting | bytes 27648 | tf_op args[6]
  16.4 0.2 reshape.95
  16.6 0.1 copy.30
  16.7 0.1 pad.25.clone
  16.8 0.0 copy-start.5
  16.8 0.4 reshape.96.refs_9_
  17.2 0.3 copy-done.5
  17.5 0.1 copy.19
  17.6 0.2 copy.29
  17.7 0.0 copy-start.2
  17.7 0.0 copy-start.6
  17.8 0.1 reshape.94.refs_5_
  17.9 0.6 copy-done.6
  18.4 0.0 collective-permute-done.2.far_0
  18.4 0.1 collective-permute-done.3.far_1
  18.5 0.0 collective-permute-done.near_0
  18.5 0.0 collective-permute-done.1.near_1
  18.5 0.6 shard_map.135
  19.1 0.1 collective-permute-start.4
  19.2 3.6 %collective-permute-start.5 = (f32[70,256]{1,0:T(8,128)S(1)}, f32[70,256]{1,0:T(8,128)S(1)}, u32[]{:S(2)}, u32[]{:S(2)}) collective-permute-start(f32[70,256]{1,0:T(8,128)S(1)} %get-tuple-element.47), channel_id=1, source_target_pairs={{0,15},{1,2},{2,1},{3,4},{4,3},{5,6},{6,5},{7,8},{8,7},{9,10},{10,... | collective-permute-start | bytes 215048 | tf_op jit(solution)/shard_map/ppermute | solution.py:673
  22.8 0.0 copy-done.2
  22.8 0.2 copy.25
  23.0 0.1 copy.26
  23.1 0.2 reshape.100
  23.3 0.7 %copy-done.3 = f32[16,8,2,2,2]{0,4,3,2,1:T(2,128)S(1)} copy-done((f32[16,8,2,2,2]{0,4,3,2,1:T(2,128)S(1)}, f32[16,8,2,2,2]{0,4,3,2,1:T(2,128)}, u32[]{:S(2)}) %copy-start.3) | copy-done | bytes 4120
  24.0 0.0 copy-start.4
  24.1 0.1 copy.28.refs_6_
  24.1 0.7 copy-done.4
  24.8 0.0 collective-permute-done.4.refs_2_
  24.9 0.6 collective-permute-done.5.refs_3_
  25.5 0.1 copy-done.1
  25.6 10.9 %shard_map.136 = (f32[2,128,256]{2,1,0:T(8,128)S(1)}, f32[120,128]{1,0:T(8,128)S(1)}) custom-call(s32[2]{0:T(128)S(1)} %pad_add_fusion.pos.refs_0_, f32[14,8,256]{2,1,0:T(8,128)S(1)} %get-tuple-element.45.refs_1_, f32[70,256]{1,0:T(8,128)S(1)} %collective-permute-done.4.refs_2_, f32[70,256]{1,0:T(8,128)S(1)} %collective-permute-done.5.refs_3_, ...), custom_call_target="tpu_custom_call" | custom-call | flops 3000000000 | bytes 2000000 | tf_op jit(solution)/shard_map/pallas_call | solution.py:656
  36.5 0.1 collective-permute-start.6
  36.6 0.3 collective-permute-start.7
  37.0 1.5 %collective-permute-start.8 = (f32[120,128]{1,0:T(8,128)S(1)}, f32[120,128]{1,0:T(8,128)S(1)}, u32[]{:S(2)}, u32[]{:S(2)}) collective-permute-start(f32[120,128]{1,0:T(8,128)S(1)} %get-tuple-element.57), channel_id=1, source_target_pairs={{0,3},{1,2},{2,1},{3,0},{4,7},{5,6},{6,5},{7,4},{8,11},{9,10},{10,... | collective-permute-start | bytes 184328 | tf_op jit(solution)/shard_map/ppermute | solution.py:733
  38.5 0.0 collective-permute-done.6
  38.5 3.0 %collective-permute-done.7 = f32[120,128]{1,0:T(8,128)S(1)} collective-permute-done((f32[120,128]{1,0:T(8,128)S(1)}, f32[120,128]{1,0:T(8,128)S(1)}, u32[]{:S(2)}, u32[]{:S(2)}) %collective-permute-start.7) | collective-permute-done | bytes 61472 | tf_op jit(solution)/shard_map/ppermute | solution.py:733
  41.5 0.4 collective-permute-done.8
  41.9 2.3 %collective-permute-start.10 = (f32[120,128]{1,0:T(8,128)S(1)}, f32[120,128]{1,0:T(8,128)S(1)}, u32[]{:S(2)}, u32[]{:S(2)}) collective-permute-start(f32[120,128]{1,0:T(8,128)S(1)} %add_add_fusion.1), channel_id=1, source_target_pairs={{0,8},{1,9},{2,10},{3,11},{4,12},{5,13},{6,14},{7,15},{8,0},{9,1},... | collective-permute-start | bytes 184328 | tf_op jit(solution)/shard_map/ppermute | solution.py:733
  44.2 1.4 %collective-permute-start.11 = (f32[120,128]{1,0:T(8,128)S(1)}, f32[120,128]{1,0:T(8,128)S(1)}, u32[]{:S(2)}, u32[]{:S(2)}) collective-permute-start(f32[120,128]{1,0:T(8,128)S(1)} %add_add_fusion.1), channel_id=1, source_target_pairs={{0,12},{1,13},{2,14},{3,15},{4,8},{5,9},{6,10},{7,11},{8,4},{9,5},... | collective-permute-start | bytes 184328 | tf_op jit(solution)/shard_map/ppermute | solution.py:733
  45.6 0.4 collective-permute-start.9
  46.0 1.8 %collective-permute-done.10 = f32[120,128]{1,0:T(8,128)S(1)} collective-permute-done((f32[120,128]{1,0:T(8,128)S(1)}, f32[120,128]{1,0:T(8,128)S(1)}, u32[]{:S(2)}, u32[]{:S(2)}) %collective-permute-start.10) | collective-permute-done | bytes 61472 | tf_op jit(solution)/shard_map/ppermute | solution.py:733
  47.7 1.9 %collective-permute-done.11 = f32[120,128]{1,0:T(8,128)S(1)} collective-permute-done((f32[120,128]{1,0:T(8,128)S(1)}, f32[120,128]{1,0:T(8,128)S(1)}, u32[]{:S(2)}, u32[]{:S(2)}) %collective-permute-start.11) | collective-permute-done | bytes 61472 | tf_op jit(solution)/shard_map/ppermute | solution.py:733
  49.6 0.2 collective-permute-done.9
  49.9 2.2 %collective-permute-start.12 = (f32[120,128]{1,0:T(8,128)S(1)}, f32[120,128]{1,0:T(8,128)S(1)}, u32[]{:S(2)}, u32[]{:S(2)}) collective-permute-start(f32[120,128]{1,0:T(8,128)S(1)} %add_add_fusion), channel_id=1, source_target_pairs={{0,16},{16,0},{32,48},{48,32},{64,80},{80,64},{96,112},{112,96},{1... | collective-permute-start | bytes 184328 | tf_op jit(solution)/shard_map/ppermute | solution.py:733
  52.1 3.9 %collective-permute-done.12 = f32[120,128]{1,0:T(8,128)S(1)} collective-permute-done((f32[120,128]{1,0:T(8,128)S(1)}, f32[120,128]{1,0:T(8,128)S(1)}, u32[]{:S(2)}, u32[]{:S(2)}) %collective-permute-start.12) | collective-permute-done | bytes 61472 | tf_op jit(solution)/shard_map/ppermute | solution.py:733
  56.0 4.8 %collective-permute-start.13 = (f32[120,128]{1,0:T(8,128)S(1)}, f32[120,128]{1,0:T(8,128)S(1)}, u32[]{:S(2)}, u32[]{:S(2)}) collective-permute-start(f32[120,128]{1,0:T(8,128)S(1)} %add.42), channel_id=1, source_target_pairs={{0,48},{16,32},{32,16},{48,0},{64,112},{80,96},{96,80},{112,64},{1... | collective-permute-start | bytes 184328 | tf_op jit(solution)/shard_map/ppermute | solution.py:733
  60.7 2.4 %collective-permute-done.13 = f32[120,128]{1,0:T(8,128)S(1)} collective-permute-done((f32[120,128]{1,0:T(8,128)S(1)}, f32[120,128]{1,0:T(8,128)S(1)}, u32[]{:S(2)}, u32[]{:S(2)}) %collective-permute-start.13) | collective-permute-done | bytes 61472 | tf_op jit(solution)/shard_map/ppermute | solution.py:733
  63.2 0.1 collective-permute-start.14
  63.3 3.6 %collective-permute-start.15 = (f32[120,128]{1,0:T(8,128)S(1)}, f32[120,128]{1,0:T(8,128)S(1)}, u32[]{:S(2)}, u32[]{:S(2)}) collective-permute-start(f32[120,128]{1,0:T(8,128)S(1)} %add.43.refs_0_), channel_id=1, source_target_pairs={{0,128},{16,144},{32,160},{48,176},{64,192},{80,208},{96,224},{112... | collective-permute-start | bytes 184328 | tf_op jit(solution)/shard_map/ppermute | solution.py:733
  66.9 1.0 %collective-permute-start.16 = (f32[120,128]{1,0:T(8,128)S(1)}, f32[120,128]{1,0:T(8,128)S(1)}, u32[]{:S(2)}, u32[]{:S(2)}) collective-permute-start(f32[120,128]{1,0:T(8,128)S(1)} %add.43.refs_0_), channel_id=1, source_target_pairs={{0,192},{16,208},{32,224},{48,240},{64,128},{80,144},{96,160},{112... | collective-permute-start | bytes 184328 | tf_op jit(solution)/shard_map/ppermute | solution.py:733
  67.9 1.2 %shard_map.137 = f32[4,8,256]{2,1,0:T(8,128)} custom-call(f32[2,128,256]{2,1,0:T(8,128)S(1)} %get-tuple-element.56.act_own, f32[1,128]{1,0:T(1,128)S(1)} %pad.26.refs_10_.w_last), custom_call_target="tpu_custom_call" | custom-call | flops 200000000 | bytes 400000 | tf_op jit(solution)/shard_map/pallas_call | solution.py:564
  69.1 0.0 collective-permute-done.14.refs_1_
  69.1 0.6 collective-permute-done.15.refs_2_
  69.8 2.6 %collective-permute-done.16.refs_3_ = f32[120,128]{1,0:T(8,128)S(1)} collective-permute-done((f32[120,128]{1,0:T(8,128)S(1)}, f32[120,128]{1,0:T(8,128)S(1)}, u32[]{:S(2)}, u32[]{:S(2)}) %collective-permute-start.16) | collective-permute-done | bytes 61472 | tf_op jit(solution)/shard_map/ppermute | solution.py:733
  72.3 0.8 %shard_map.138 = (f32[16,16,27]{2,1,0:T(8,128)}, f32[8,16,27]{2,1,0:T(8,128)}, f32[8,1,27]{2,1,0:T(1,128)}, f32[8,4,2,16]{3,2,1,0:T(2,128)}, f32[8,4,2,16]{3,2,1,0:T(2,128)}, /*index=5*/f32[1,8]{1,0:T(1,128)}) custom-call(f32[120,128]{1,0:T(8,128)S(1)} %add.43.refs_0_, f32[120,128]{1,0:T(8,128)S(1)} %collective-permute-done.14.refs_1_, ...), custom_call_target="tpu_custom_call" | custom-call | tf_op jit(solution)/shard_map/pallas_call | solution.py:614
  (14 shorter events, 0.1 us)
Async XLA Ops:
  0.6 0.8 %copy-start = (f32[1,4,8,256]{3,2,1,0:T(8,128)S(1)}, f32[1,4,8,256]{3,2,1,0:T(8,128)}, u32[]{:S(2)}) copy-start(f32[1,4,8,256]{3,2,1,0:T(8,128)} %param.8) | copy-start | bytes 98308
  1.4 17.1 %collective-permute-start = (f32[4,8,256]{2,1,0:T(8,128)S(1)}, f32[4,8,256]{2,1,0:T(8,128)S(1)}, u32[]{:S(2)}, u32[]{:S(2)}) collective-permute-start(f32[4,8,256]{2,1,0:T(8,128)S(1)} %bitcast.30), channel_id=1, source_target_pairs={{0,16},{16,0},{32,48},{48,32},{64,80},{80,64},{96,112},{112,96},{1... | collective-permute-start | bytes 98312 | tf_op jit(solution)/shard_map/ppermute | solution.py:673
  4.7 13.9 %collective-permute-start.1 = (f32[4,8,256]{2,1,0:T(8,128)S(1)}, f32[4,8,256]{2,1,0:T(8,128)S(1)}, u32[]{:S(2)}, u32[]{:S(2)}) collective-permute-start(f32[4,8,256]{2,1,0:T(8,128)S(1)} %bitcast.31), channel_id=1, source_target_pairs={{0,240},{16,32},{32,16},{48,64},{64,48},{80,96},{96,80},{112,128},... | collective-permute-start | bytes 98312 | tf_op jit(solution)/shard_map/ppermute | solution.py:673
  9.4 9.0 %collective-permute-start.2 = (f32[1,8,256]{2,1,0:T(8,128)S(1)}, f32[1,8,256]{2,1,0:T(8,128)S(1)}, u32[]{:S(2)}, u32[]{:S(2)}) collective-permute-start(f32[1,8,256]{2,1,0:T(8,128)S(1)} %get-tuple-element.38), channel_id=1, source_target_pairs={{0,32},{16,48},{32,0},{48,16},{64,96},{80,112},{96,64},{112,80},{1... | collective-permute-start | bytes 24584 | tf_op jit(solution)/shard_map/ppermute | solution.py:673
  10.1 8.5 %collective-permute-start.3 = (f32[1,8,256]{2,1,0:T(8,128)S(1)}, f32[1,8,256]{2,1,0:T(8,128)S(1)}, u32[]{:S(2)}, u32[]{:S(2)}) collective-permute-start(f32[1,8,256]{2,1,0:T(8,128)S(1)} %get-tuple-element.39), channel_id=1, source_target_pairs={{0,224},{16,240},{32,64},{48,80},{64,32},{80,48},{96,128},{112,144... | collective-permute-start | bytes 24584 | tf_op jit(solution)/shard_map/ppermute | solution.py:673
  16.8 0.7 copy-start.5
  17.7 5.1 %copy-start.2 = (f32[27,16,16]{0,2,1:T(8,128)S(1)}, f32[27,16,16]{0,2,1:T(8,128)}, u32[]{:S(2)}) copy-start(f32[27,16,16]{0,2,1:T(8,128)} %param.12) | copy-start | bytes 82948
  17.7 0.7 copy-start.6
  19.1 5.7 %collective-permute-start.4 = (f32[70,256]{1,0:T(8,128)S(1)}, f32[70,256]{1,0:T(8,128)S(1)}, u32[]{:S(2)}, u32[]{:S(2)}) collective-permute-start(f32[70,256]{1,0:T(8,128)S(1)} %get-tuple-element.46), channel_id=1, source_target_pairs={{0,1},{1,0},{2,3},{3,2},{4,5},{5,4},{6,7},{7,6},{8,9},{9,8},{10,11... | collective-permute-start | bytes 215048 | tf_op jit(solution)/shard_map/ppermute | solution.py:673
  19.2 6.2 %collective-permute-start.5 = (f32[70,256]{1,0:T(8,128)S(1)}, f32[70,256]{1,0:T(8,128)S(1)}, u32[]{:S(2)}, u32[]{:S(2)}) collective-permute-start(f32[70,256]{1,0:T(8,128)S(1)} %get-tuple-element.47), channel_id=1, source_target_pairs={{0,15},{1,2},{2,1},{3,4},{4,3},{5,6},{6,5},{7,8},{8,7},{9,10},{10,... | collective-permute-start | bytes 215048 | tf_op jit(solution)/shard_map/ppermute | solution.py:673
  23.3 0.8 %copy-start.3 = (f32[16,8,2,2,2]{0,4,3,2,1:T(2,128)S(1)}, f32[16,8,2,2,2]{0,4,3,2,1:T(2,128)}, u32[]{:S(2)}) copy-start(f32[16,8,2,2,2]{0,4,3,2,1:T(2,128)} %param.11) | copy-start | bytes 12292
  24.0 0.8 %copy-start.4 = (f32[8,16,2,2,2]{1,4,3,2,0:T(2,128)S(1)}, f32[8,16,2,2,2]{1,4,3,2,0:T(2,128)}, u32[]{:S(2)}) copy-start(f32[8,16,2,2,2]{1,4,3,2,0:T(2,128)} %param.13) | copy-start | bytes 12292
  24.8 0.8 %copy-start.1 = (f32[1,4,8,256]{3,2,1,0:T(8,128)S(1)}, f32[1,4,8,256]{3,2,1,0:T(8,128)}, u32[]{:S(2)}) copy-start(f32[1,4,8,256]{3,2,1,0:T(8,128)} %param.9) | copy-start | bytes 98308
  36.5 2.0 %collective-permute-start.6 = (f32[120,128]{1,0:T(8,128)S(1)}, f32[120,128]{1,0:T(8,128)S(1)}, u32[]{:S(2)}, u32[]{:S(2)}) collective-permute-start(f32[120,128]{1,0:T(8,128)S(1)} %get-tuple-element.57), channel_id=1, source_target_pairs={{0,1},{1,0},{2,3},{3,2},{4,5},{5,4},{6,7},{7,6},{8,9},{9,8},{10,11... | collective-permute-start | bytes 184328 | tf_op jit(solution)/shard_map/ppermute | solution.py:733
  36.6 4.9 %collective-permute-start.7 = (f32[120,128]{1,0:T(8,128)S(1)}, f32[120,128]{1,0:T(8,128)S(1)}, u32[]{:S(2)}, u32[]{:S(2)}) collective-permute-start(f32[120,128]{1,0:T(8,128)S(1)} %get-tuple-element.57), channel_id=1, source_target_pairs={{0,2},{1,3},{2,0},{3,1},{4,6},{5,7},{6,4},{7,5},{8,10},{9,11},{10,... | collective-permute-start | bytes 184328 | tf_op jit(solution)/shard_map/ppermute | solution.py:733
  37.0 4.9 %collective-permute-start.8 = (f32[120,128]{1,0:T(8,128)S(1)}, f32[120,128]{1,0:T(8,128)S(1)}, u32[]{:S(2)}, u32[]{:S(2)}) collective-permute-start(f32[120,128]{1,0:T(8,128)S(1)} %get-tuple-element.57), channel_id=1, source_target_pairs={{0,3},{1,2},{2,1},{3,0},{4,7},{5,6},{6,5},{7,4},{8,11},{9,10},{10,... | collective-permute-start | bytes 184328 | tf_op jit(solution)/shard_map/ppermute | solution.py:733
  41.9 5.8 %collective-permute-start.10 = (f32[120,128]{1,0:T(8,128)S(1)}, f32[120,128]{1,0:T(8,128)S(1)}, u32[]{:S(2)}, u32[]{:S(2)}) collective-permute-start(f32[120,128]{1,0:T(8,128)S(1)} %add_add_fusion.1), channel_id=1, source_target_pairs={{0,8},{1,9},{2,10},{3,11},{4,12},{5,13},{6,14},{7,15},{8,0},{9,1},... | collective-permute-start | bytes 184328 | tf_op jit(solution)/shard_map/ppermute | solution.py:733
  44.2 5.4 %collective-permute-start.11 = (f32[120,128]{1,0:T(8,128)S(1)}, f32[120,128]{1,0:T(8,128)S(1)}, u32[]{:S(2)}, u32[]{:S(2)}) collective-permute-start(f32[120,128]{1,0:T(8,128)S(1)} %add_add_fusion.1), channel_id=1, source_target_pairs={{0,12},{1,13},{2,14},{3,15},{4,8},{5,9},{6,10},{7,11},{8,4},{9,5},... | collective-permute-start | bytes 184328 | tf_op jit(solution)/shard_map/ppermute | solution.py:733
  45.6 4.2 %collective-permute-start.9 = (f32[120,128]{1,0:T(8,128)S(1)}, f32[120,128]{1,0:T(8,128)S(1)}, u32[]{:S(2)}, u32[]{:S(2)}) collective-permute-start(f32[120,128]{1,0:T(8,128)S(1)} %add_add_fusion.1), channel_id=1, source_target_pairs={{0,4},{1,5},{2,6},{3,7},{4,0},{5,1},{6,2},{7,3},{8,12},{9,13},{10,... | collective-permute-start | bytes 184328 | tf_op jit(solution)/shard_map/ppermute | solution.py:733
  49.9 6.1 %collective-permute-start.12 = (f32[120,128]{1,0:T(8,128)S(1)}, f32[120,128]{1,0:T(8,128)S(1)}, u32[]{:S(2)}, u32[]{:S(2)}) collective-permute-start(f32[120,128]{1,0:T(8,128)S(1)} %add_add_fusion), channel_id=1, source_target_pairs={{0,16},{16,0},{32,48},{48,32},{64,80},{80,64},{96,112},{112,96},{1... | collective-permute-start | bytes 184328 | tf_op jit(solution)/shard_map/ppermute | solution.py:733
  56.0 7.2 %collective-permute-start.13 = (f32[120,128]{1,0:T(8,128)S(1)}, f32[120,128]{1,0:T(8,128)S(1)}, u32[]{:S(2)}, u32[]{:S(2)}) collective-permute-start(f32[120,128]{1,0:T(8,128)S(1)} %add.42), channel_id=1, source_target_pairs={{0,48},{16,32},{32,16},{48,0},{64,112},{80,96},{96,80},{112,64},{1... | collective-permute-start | bytes 184328 | tf_op jit(solution)/shard_map/ppermute | solution.py:733
  63.2 6.0 %collective-permute-start.14 = (f32[120,128]{1,0:T(8,128)S(1)}, f32[120,128]{1,0:T(8,128)S(1)}, u32[]{:S(2)}, u32[]{:S(2)}) collective-permute-start(f32[120,128]{1,0:T(8,128)S(1)} %add.43.refs_0_), channel_id=1, source_target_pairs={{0,64},{16,80},{32,96},{48,112},{64,0},{80,16},{96,32},{112,48},{1... | collective-permute-start | bytes 184328 | tf_op jit(solution)/shard_map/ppermute | solution.py:733
  63.3 6.5 %collective-permute-start.15 = (f32[120,128]{1,0:T(8,128)S(1)}, f32[120,128]{1,0:T(8,128)S(1)}, u32[]{:S(2)}, u32[]{:S(2)}) collective-permute-start(f32[120,128]{1,0:T(8,128)S(1)} %add.43.refs_0_), channel_id=1, source_target_pairs={{0,128},{16,144},{32,160},{48,176},{64,192},{80,208},{96,224},{112... | collective-permute-start | bytes 184328 | tf_op jit(solution)/shard_map/ppermute | solution.py:733
  66.9 5.4 %collective-permute-start.16 = (f32[120,128]{1,0:T(8,128)S(1)}, f32[120,128]{1,0:T(8,128)S(1)}, u32[]{:S(2)}, u32[]{:S(2)}) collective-permute-start(f32[120,128]{1,0:T(8,128)S(1)} %add.43.refs_0_), channel_id=1, source_target_pairs={{0,192},{16,208},{32,224},{48,240},{64,128},{80,144},{96,160},{112... | collective-permute-start | bytes 184328 | tf_op jit(solution)/shard_map/ppermute | solution.py:733

commit v3 on v2

--- a/solution.py
+++ b/solution.py
@@ -536,6 +536,7 @@
     )
     lane, row = lane_of((8, 128)), lax.broadcasted_iota(jnp.int32, (8, 128), 0)
     pay[112:120] = part_first + jnp.where(lane == 64 + row, part_final, 0.0)
+    pay[120:128] = jnp.zeros((8, 128), F32)
 
 
 def image(act_own, w_last, img):
@@ -585,12 +586,9 @@
     return sum(roll(found[count * dx : count * dx + count], 9 * dx) for dx in range(len(parts)))
 
 
-def outputs(*refs):
-    blocks, (coarse, joined, first, down, up, final) = refs[:-6], refs[-6:]
-    total = [ref[...] for ref in blocks]
-    while len(total) > 1:
-        total = [total[i] + total[i + 1] for i in range(0, len(total), 2)]
-    total = total[0]
+def outputs(pos, mine, other, coarse, joined, first, down, up, final):
+    lower = (pos[1] & 1) == 0
+    total = rows([jnp.where(lower, mine[...], other[...]), jnp.where(lower, other[...], mine[...])])
 
     def slot(start, count, at, width):
         block = total[start : start + count]
@@ -608,16 +606,22 @@
     final[...] = roll(row_sum, -64)[:, :8]
 
 
-def run_outputs(blocks):
+def summed(blocks):
+    while len(blocks) > 1:
+        blocks = [blocks[i] + blocks[i + 1] for i in range(0, len(blocks), 2)]
+    return blocks[0]
+
+
+def run_outputs(*args):
     vmem = pl.BlockSpec(memory_space=pltpu.VMEM)
     shapes = ((16, 16, 27), (8, 16, 27), (8, 1, 27), (8, 4, 2, 16), (8, 4, 2, 16), (1, 8))
     return pl.pallas_call(
         outputs,
         out_shape=tuple(jax.ShapeDtypeStruct(shape, F32) for shape in shapes),
-        in_specs=[vmem] * len(blocks),
+        in_specs=[pl.BlockSpec(memory_space=pltpu.SMEM), vmem, vmem],
         out_specs=(vmem,) * len(shapes),
         compiler_params=pltpu.CompilerParams(vmem_limit_bytes=4 * 1024 * 1024),
-    )(*blocks)
+    )(*args)
 
 
 def run_kernel(args, scale, size_x, size_y):
@@ -655,7 +659,7 @@
 
     return pl.pallas_call(
         unet_tile,
-        out_shape=(jax.ShapeDtypeStruct((2, 128, 256), F32), jax.ShapeDtypeStruct((120, 128), F32)),
+        out_shape=(jax.ShapeDtypeStruct((2, 128, 256), F32), jax.ShapeDtypeStruct((128, 128), F32)),
         in_specs=[pl.BlockSpec(memory_space=pltpu.SMEM)] + [vmem] * (len(args) - 1),
         out_specs=(vmem, vmem),
         scratch_shapes=scratch,
@@ -723,18 +727,19 @@
     scale = 1.0 / math.sqrt(size_x * size_y * in_field.shape[3])
     act_own, pay = run_kernel([pos, wide, *beside, cot, *weights], scale, size_x, size_y)
 
-    blocks, imitated = [pay], None
+    block, imitated = pay, None
     for axis in ("gy", "gx"):
         count = lax.axis_size(axis)
         for partners in rounds(count, axis == "gx"):
-            while len(blocks) > 1:
-                blocks = [blocks[i] + blocks[i + 1] for i in range(0, len(blocks), 2)]
-            mine = blocks[0]
-            blocks = [mine] + [lax.ppermute(mine, axis, [(i, i ^ k) for i in range(count)]) for k in partners]
+            blocks = [block] + [lax.ppermute(block, axis, [(i, i ^ k) for i in range(count)]) for k in partners]
             if imitated is None:
                 act_own, blocks = lax.optimization_barrier((act_own, blocks))
                 imitated = run_image(act_own, last)
-    coarse, joined, first, down, up, final = run_outputs(blocks)
+                block = lax.dynamic_slice_in_dim(summed(blocks), 64 * (lax.axis_index("gy") & 1), 64)
+            else:
+                block = summed(blocks)
+    other = lax.ppermute(block, "gy", [(i, i ^ 1) for i in range(lax.axis_size("gy"))])
+    coarse, joined, first, down, up, final = run_outputs(pos, block, other)
     return (
         imitated[None],
         first.transpose(2, 0, 1),

time: 73.6 us -> 76 us (1.033)
  the two profiles are of different devices: /device:TPU:6 before, /device:TPU:1 now
where the time goes in v3:
time: 76 us; the launch traced here: 75.5 us
  starting transfers between devices  39.7 us (52%)
  waiting for transfers between devices  15.1 us (20%)
  Pallas kernels  14.1 us (19%)
  local copies, waits for them, and re-layouts  4.99 us (7%)
  other arithmetic  0.87 us (1%)
  between operations  0.82 us (1%)
    ppermute x11, starting transfers between devices, shards(): lax.ppermute(block, axis, [(i, i ^ k) for i in range(count)])  15.3 us
    ppermute x11, waiting for transfers between devices, shards(): lax.ppermute(block, axis, [(i, i ^ k) for i in range(count)])  14 us
    ppermute x3, starting transfers between devices, swap(): lax.ppermute(second, axis, pairs(1))  12.9 us
    pallas_call x1, Pallas kernels, run_kernel(): pl.pallas_call(unet_tile, out_shape=(jax.ShapeDtypeStruct((2, 128, 256),...  10.9 us
    ppermute x3, starting transfers between devices, swap(): lax.ppermute(first, axis, pairs(0))  6.04 us
    ppermute x1, starting transfers between devices, shards(): lax.ppermute(block, 'gy', [(i, i ^ 1) for i in range(lax.axis_size('gy'))])  5.45 us
    unnamed x18, local copies, waits for them, and re-layouts  3.66 us
  transfers between devices with their start and end apart: 18, of which 9 were waited for; matrix products, arithmetic and copies ran while one was open for 4% of the time, Pallas kernels for 2%

profile of v3, /device:TPU:1, one launch (start us, length us, event | category | flops | bytes accessed | tf_op | source)
XLA Modules:
  0.0 75.5 jit_solution(7105047155645275352)
XLA Ops:
  0.6 0.0 copy-start
  0.7 0.8 %select_bitcast_fusion = (f32[1,8,256]{2,1,0:T(8,128)S(1)}, f32[1,8,256]{2,1,0:T(8,128)S(1)}) fusion(f32[1,4,8,256]{3,2,1,0:T(8,128)} %param.8, pred[]{:T(512)S(6)} %eq.3), kind=kLoop, calls=%fused_computation.5 | loop fusion | flops 4096 | bytes 32769 | tf_op jit(solution)/shard_map/jit(_where)/select_n | solution.py:714
  1.4 0.0 copy-done
  1.4 3.8 %collective-permute-start = (f32[4,8,256]{2,1,0:T(8,128)S(1)}, f32[4,8,256]{2,1,0:T(8,128)S(1)}, u32[]{:S(2)}, u32[]{:S(2)}) collective-permute-start(f32[4,8,256]{2,1,0:T(8,128)S(1)} %bitcast.30), channel_id=1, source_target_pairs={{0,16},{16,0},{32,48},{48,32},{64,80},{80,64},{96,112},{112,96},{1... | collective-permute-start | bytes 98312 | tf_op jit(solution)/shard_map/ppermute | solution.py:677
  5.2 6.4 %collective-permute-start.1 = (f32[4,8,256]{2,1,0:T(8,128)S(1)}, f32[4,8,256]{2,1,0:T(8,128)S(1)}, u32[]{:S(2)}, u32[]{:S(2)}) collective-permute-start(f32[4,8,256]{2,1,0:T(8,128)S(1)} %bitcast.31), channel_id=1, source_target_pairs={{0,240},{16,32},{32,16},{48,64},{64,48},{80,96},{96,80},{112,128},... | collective-permute-start | bytes 98312 | tf_op jit(solution)/shard_map/ppermute | solution.py:677
  11.6 0.0 collective-permute-start.2
  11.6 5.6 %collective-permute-start.3 = (f32[1,8,256]{2,1,0:T(8,128)S(1)}, f32[1,8,256]{2,1,0:T(8,128)S(1)}, u32[]{:S(2)}, u32[]{:S(2)}) collective-permute-start(f32[1,8,256]{2,1,0:T(8,128)S(1)} %get-tuple-element.39), channel_id=1, source_target_pairs={{0,224},{16,240},{32,64},{48,80},{64,32},{80,48},{96,128},{112,144... | collective-permute-start | bytes 24584 | tf_op jit(solution)/shard_map/ppermute | solution.py:677
  17.3 0.1 pad_add_fusion.pos.refs_0_
  17.3 1.0 %copy.21 = f32[27,8,16]{2,1,0:T(8,128)S(1)} copy(f32[27,8,16]{0,2,1:T(8,128)} %param.14) | data formatting | bytes 27648 | tf_op args[6]
  18.3 0.2 reshape.95
  18.5 0.1 copy.30
  18.6 0.1 pad.25.clone
  18.7 0.0 copy-start.5
  18.7 0.4 reshape.96.refs_9_
  19.1 0.3 copy-done.5
  19.4 0.1 copy.19
  19.5 0.2 copy.29
  19.7 0.0 copy-start.6
  19.7 0.1 reshape.94.refs_5_
  19.8 0.6 copy-done.6
  20.4 0.0 collective-permute-done.2.far_0
  20.4 0.0 collective-permute-done.3.far_1
  20.4 0.0 collective-permute-done.near_0
  20.4 0.0 collective-permute-done.1.near_1
  20.4 0.6 shard_map.135
  21.0 2.2 %collective-permute-start.4 = (f32[70,256]{1,0:T(8,128)S(1)}, f32[70,256]{1,0:T(8,128)S(1)}, u32[]{:S(2)}, u32[]{:S(2)}) collective-permute-start(f32[70,256]{1,0:T(8,128)S(1)} %get-tuple-element.46), channel_id=1, source_target_pairs={{0,1},{1,0},{2,3},{3,2},{4,5},{5,4},{6,7},{7,6},{8,9},{9,8},{10,11... | collective-permute-start | bytes 215048 | tf_op jit(solution)/shard_map/ppermute | solution.py:677
  23.2 0.9 %collective-permute-start.5 = (f32[70,256]{1,0:T(8,128)S(1)}, f32[70,256]{1,0:T(8,128)S(1)}, u32[]{:S(2)}, u32[]{:S(2)}) collective-permute-start(f32[70,256]{1,0:T(8,128)S(1)} %get-tuple-element.47), channel_id=1, source_target_pairs={{0,15},{1,2},{2,1},{3,4},{4,3},{5,6},{6,5},{7,8},{8,7},{9,10},{10,... | collective-permute-start | bytes 215048 | tf_op jit(solution)/shard_map/ppermute | solution.py:677
  24.1 0.0 copy-done.2
  24.1 0.2 copy.25
  24.3 0.1 copy.26
  24.4 0.2 reshape.100
  24.6 0.7 copy-done.3
  25.4 0.0 copy-start.4
  25.4 0.1 copy.28.refs_6_
  25.4 0.7 copy-done.4
  26.2 0.0 collective-permute-done.4.refs_2_
  26.2 1.1 %collective-permute-done.5.refs_3_ = f32[70,256]{1,0:T(8,128)S(1)} collective-permute-done((f32[70,256]{1,0:T(8,128)S(1)}, f32[70,256]{1,0:T(8,128)S(1)}, u32[]{:S(2)}, u32[]{:S(2)}) %collective-permute-start.5) | collective-permute-done | bytes 71712 | tf_op jit(solution)/shard_map/ppermute | solution.py:677
  27.2 10.9 %shard_map.136 = (f32[2,128,256]{2,1,0:T(8,128)S(1)}, f32[128,128]{1,0:T(8,128)S(1)}) custom-call(s32[2]{0:T(128)S(1)} %pad_add_fusion.pos.refs_0_, f32[14,8,256]{2,1,0:T(8,128)S(1)} %get-tuple-element.45.refs_1_, f32[70,256]{1,0:T(8,128)S(1)} %collective-permute-done.4.refs_2_, f32[70,256]{1,0:T(8,128)S(1)} %collective-permute-done.5.refs_3_, ...), custom_call_target="tpu_custom_call" | custom-call | flops 3000000000 | bytes 2000000 | tf_op jit(solution)/shard_map/pallas_call | solution.py:660
  38.2 2.4 %collective-permute-start.6 = (f32[128,128]{1,0:T(8,128)S(1)}, f32[128,128]{1,0:T(8,128)S(1)}, u32[]{:S(2)}, u32[]{:S(2)}) collective-permute-start(f32[128,128]{1,0:T(8,128)S(1)} %get-tuple-element.57), channel_id=1, source_target_pairs={{0,1},{1,0},{2,3},{3,2},{4,5},{5,4},{6,7},{7,6},{8,9},{9,8},{10,11... | collective-permute-start | bytes 196616 | tf_op jit(solution)/shard_map/ppermute | solution.py:734
  40.6 0.0 collective-permute-start.7
  40.6 1.7 %collective-permute-start.8 = (f32[128,128]{1,0:T(8,128)S(1)}, f32[128,128]{1,0:T(8,128)S(1)}, u32[]{:S(2)}, u32[]{:S(2)}) collective-permute-start(f32[128,128]{1,0:T(8,128)S(1)} %get-tuple-element.57), channel_id=1, source_target_pairs={{0,3},{1,2},{2,1},{3,0},{4,7},{5,6},{6,5},{7,4},{8,11},{9,10},{10,... | collective-permute-start | bytes 196616 | tf_op jit(solution)/shard_map/ppermute | solution.py:734
  42.4 0.0 collective-permute-done.6
  42.4 1.9 %collective-permute-done.7 = f32[128,128]{1,0:T(8,128)S(1)} collective-permute-done((f32[128,128]{1,0:T(8,128)S(1)}, f32[128,128]{1,0:T(8,128)S(1)}, u32[]{:S(2)}, u32[]{:S(2)}) %collective-permute-start.7) | collective-permute-done | bytes 65568 | tf_op jit(solution)/shard_map/ppermute | solution.py:734
  44.3 1.6 %collective-permute-done.8 = f32[128,128]{1,0:T(8,128)S(1)} collective-permute-done((f32[128,128]{1,0:T(8,128)S(1)}, f32[128,128]{1,0:T(8,128)S(1)}, u32[]{:S(2)}, u32[]{:S(2)}) %collective-permute-start.8) | collective-permute-done | bytes 65568 | tf_op jit(solution)/shard_map/ppermute | solution.py:734
  45.9 1.8 %collective-permute-start.10 = (f32[64,128]{1,0:T(8,128)S(1)}, f32[64,128]{1,0:T(8,128)S(1)}, u32[]{:S(2)}, u32[]{:S(2)}) collective-permute-start(f32[64,128]{1,0:T(8,128)S(1)} %fusion), channel_id=1, source_target_pairs={{0,8},{1,9},{2,10},{3,11},{4,12},{5,13},{6,14},{7,15},{8,0},{9,1},... | collective-permute-start | bytes 98312 | tf_op jit(solution)/shard_map/ppermute | solution.py:734
  47.7 1.1 %collective-permute-start.11 = (f32[64,128]{1,0:T(8,128)S(1)}, f32[64,128]{1,0:T(8,128)S(1)}, u32[]{:S(2)}, u32[]{:S(2)}) collective-permute-start(f32[64,128]{1,0:T(8,128)S(1)} %fusion), channel_id=1, source_target_pairs={{0,12},{1,13},{2,14},{3,15},{4,8},{5,9},{6,10},{7,11},{8,4},{9,5},... | collective-permute-start | bytes 98312 | tf_op jit(solution)/shard_map/ppermute | solution.py:734
  48.7 0.3 collective-permute-start.9
  49.1 1.2 %collective-permute-done.10 = f32[64,128]{1,0:T(8,128)S(1)} collective-permute-done((f32[64,128]{1,0:T(8,128)S(1)}, f32[64,128]{1,0:T(8,128)S(1)}, u32[]{:S(2)}, u32[]{:S(2)}) %collective-permute-start.10) | collective-permute-done | bytes 32800 | tf_op jit(solution)/shard_map/ppermute | solution.py:734
  50.2 1.4 %collective-permute-done.11 = f32[64,128]{1,0:T(8,128)S(1)} collective-permute-done((f32[64,128]{1,0:T(8,128)S(1)}, f32[64,128]{1,0:T(8,128)S(1)}, u32[]{:S(2)}, u32[]{:S(2)}) %collective-permute-start.11) | collective-permute-done | bytes 32800 | tf_op jit(solution)/shard_map/ppermute | solution.py:734
  51.6 0.0 collective-permute-done.9
  51.7 1.7 %collective-permute-start.12 = (f32[64,128]{1,0:T(8,128)S(1)}, f32[64,128]{1,0:T(8,128)S(1)}, u32[]{:S(2)}, u32[]{:S(2)}) collective-permute-start(f32[64,128]{1,0:T(8,128)S(1)} %add_add_fusion.1), channel_id=1, source_target_pairs={{0,16},{16,0},{32,48},{48,32},{64,80},{80,64},{96,112},{112,96},{1... | collective-permute-start | bytes 98312 | tf_op jit(solution)/shard_map/ppermute | solution.py:734
  53.3 2.3 %collective-permute-done.12 = f32[64,128]{1,0:T(8,128)S(1)} collective-permute-done((f32[64,128]{1,0:T(8,128)S(1)}, f32[64,128]{1,0:T(8,128)S(1)}, u32[]{:S(2)}, u32[]{:S(2)}) %collective-permute-start.12) | collective-permute-done | bytes 32800 | tf_op jit(solution)/shard_map/ppermute | solution.py:734
  55.6 2.4 %collective-permute-start.13 = (f32[64,128]{1,0:T(8,128)S(1)}, f32[64,128]{1,0:T(8,128)S(1)}, u32[]{:S(2)}, u32[]{:S(2)}) collective-permute-start(f32[64,128]{1,0:T(8,128)S(1)} %add.55), channel_id=1, source_target_pairs={{0,48},{16,32},{32,16},{48,0},{64,112},{80,96},{96,80},{112,64},{1... | collective-permute-start | bytes 98312 | tf_op jit(solution)/shard_map/ppermute | solution.py:734
  58.0 2.5 %collective-permute-done.13 = f32[64,128]{1,0:T(8,128)S(1)} collective-permute-done((f32[64,128]{1,0:T(8,128)S(1)}, f32[64,128]{1,0:T(8,128)S(1)}, u32[]{:S(2)}, u32[]{:S(2)}) %collective-permute-start.13) | collective-permute-done | bytes 32800 | tf_op jit(solution)/shard_map/ppermute | solution.py:734
  60.5 0.6 collective-permute-start.14
  61.1 2.4 %collective-permute-start.15 = (f32[64,128]{1,0:T(8,128)S(1)}, f32[64,128]{1,0:T(8,128)S(1)}, u32[]{:S(2)}, u32[]{:S(2)}) collective-permute-start(f32[64,128]{1,0:T(8,128)S(1)} %add.56), channel_id=1, source_target_pairs={{0,128},{16,144},{32,160},{48,176},{64,192},{80,208},{96,224},{112... | collective-permute-start | bytes 98312 | tf_op jit(solution)/shard_map/ppermute | solution.py:734
  63.5 0.9 %collective-permute-start.16 = (f32[64,128]{1,0:T(8,128)S(1)}, f32[64,128]{1,0:T(8,128)S(1)}, u32[]{:S(2)}, u32[]{:S(2)}) collective-permute-start(f32[64,128]{1,0:T(8,128)S(1)} %add.56), channel_id=1, source_target_pairs={{0,192},{16,208},{32,224},{48,240},{64,128},{80,144},{96,160},{112... | collective-permute-start | bytes 98312 | tf_op jit(solution)/shard_map/ppermute | solution.py:734
  64.4 0.0 collective-permute-done.14
  64.4 1.0 %collective-permute-done.15 = f32[64,128]{1,0:T(8,128)S(1)} collective-permute-done((f32[64,128]{1,0:T(8,128)S(1)}, f32[64,128]{1,0:T(8,128)S(1)}, u32[]{:S(2)}, u32[]{:S(2)}) %collective-permute-start.15) | collective-permute-done | bytes 32800 | tf_op jit(solution)/shard_map/ppermute | solution.py:734
  65.4 2.1 %collective-permute-done.16 = f32[64,128]{1,0:T(8,128)S(1)} collective-permute-done((f32[64,128]{1,0:T(8,128)S(1)}, f32[64,128]{1,0:T(8,128)S(1)}, u32[]{:S(2)}, u32[]{:S(2)}) %collective-permute-start.16) | collective-permute-done | bytes 32800 | tf_op jit(solution)/shard_map/ppermute | solution.py:734
  67.5 5.4 %collective-permute-start.17 = (f32[64,128]{1,0:T(8,128)S(1)}, f32[64,128]{1,0:T(8,128)S(1)}, u32[]{:S(2)}, u32[]{:S(2)}) collective-permute-start(f32[64,128]{1,0:T(8,128)S(1)} %add_add_fusion.mine), channel_id=1, source_target_pairs={{0,1},{1,0},{2,3},{3,2},{4,5},{5,4},{6,7},{7,6},{8,9},{9,8},{10,11... | collective-permute-start | bytes 98312 | tf_op jit(solution)/shard_map/ppermute | solution.py:741
  73.0 1.2 %shard_map.137 = f32[4,8,256]{2,1,0:T(8,128)} custom-call(f32[2,128,256]{2,1,0:T(8,128)S(1)} %get-tuple-element.56.act_own, f32[1,128]{1,0:T(1,128)S(1)} %pad.26.refs_10_.w_last), custom_call_target="tpu_custom_call" | custom-call | flops 200000000 | bytes 400000 | tf_op jit(solution)/shard_map/pallas_call | solution.py:565
  74.1 0.0 collective-permute-done.17.other
  74.1 1.4 %shard_map.138 = (f32[16,16,27]{2,1,0:T(8,128)}, f32[8,16,27]{2,1,0:T(8,128)}, f32[8,1,27]{2,1,0:T(1,128)}, f32[8,4,2,16]{3,2,1,0:T(2,128)}, f32[8,4,2,16]{3,2,1,0:T(2,128)}, /*index=5*/f32[1,8]{1,0:T(1,128)}) custom-call(s32[2]{0:T(128)S(1)} %pad_add_fusion.pos.refs_0_, f32[64,128]{1,0:T(8,128)S(1)} %add_add_fusion.mine, ...), custom_call_target="tpu_custom_call" | custom-call | tf_op jit(solution)/shard_map/pallas_call | solution.py:618
  (17 shorter events, 0.1 us)
Async XLA Ops:
  0.6 0.8 %copy-start = (f32[1,4,8,256]{3,2,1,0:T(8,128)S(1)}, f32[1,4,8,256]{3,2,1,0:T(8,128)}, u32[]{:S(2)}) copy-start(f32[1,4,8,256]{3,2,1,0:T(8,128)} %param.8) | copy-start | bytes 98308
  1.4 19.0 %collective-permute-start = (f32[4,8,256]{2,1,0:T(8,128)S(1)}, f32[4,8,256]{2,1,0:T(8,128)S(1)}, u32[]{:S(2)}, u32[]{:S(2)}) collective-permute-start(f32[4,8,256]{2,1,0:T(8,128)S(1)} %bitcast.30), channel_id=1, source_target_pairs={{0,16},{16,0},{32,48},{48,32},{64,80},{80,64},{96,112},{112,96},{1... | collective-permute-start | bytes 98312 | tf_op jit(solution)/shard_map/ppermute | solution.py:677
  5.2 15.2 %collective-permute-start.1 = (f32[4,8,256]{2,1,0:T(8,128)S(1)}, f32[4,8,256]{2,1,0:T(8,128)S(1)}, u32[]{:S(2)}, u32[]{:S(2)}) collective-permute-start(f32[4,8,256]{2,1,0:T(8,128)S(1)} %bitcast.31), channel_id=1, source_target_pairs={{0,240},{16,32},{32,16},{48,64},{64,48},{80,96},{96,80},{112,128},... | collective-permute-start | bytes 98312 | tf_op jit(solution)/shard_map/ppermute | solution.py:677
  11.6 8.8 %collective-permute-start.2 = (f32[1,8,256]{2,1,0:T(8,128)S(1)}, f32[1,8,256]{2,1,0:T(8,128)S(1)}, u32[]{:S(2)}, u32[]{:S(2)}) collective-permute-start(f32[1,8,256]{2,1,0:T(8,128)S(1)} %get-tuple-element.38), channel_id=1, source_target_pairs={{0,32},{16,48},{32,0},{48,16},{64,96},{80,112},{96,64},{112,80},{1... | collective-permute-start | bytes 24584 | tf_op jit(solution)/shard_map/ppermute | solution.py:677
  11.6 8.8 %collective-permute-start.3 = (f32[1,8,256]{2,1,0:T(8,128)S(1)}, f32[1,8,256]{2,1,0:T(8,128)S(1)}, u32[]{:S(2)}, u32[]{:S(2)}) collective-permute-start(f32[1,8,256]{2,1,0:T(8,128)S(1)} %get-tuple-element.39), channel_id=1, source_target_pairs={{0,224},{16,240},{32,64},{48,80},{64,32},{80,48},{96,128},{112,144... | collective-permute-start | bytes 24584 | tf_op jit(solution)/shard_map/ppermute | solution.py:677
  18.7 0.7 copy-start.5
  19.7 4.5 %copy-start.2 = (f32[27,16,16]{0,2,1:T(8,128)S(1)}, f32[27,16,16]{0,2,1:T(8,128)}, u32[]{:S(2)}) copy-start(f32[27,16,16]{0,2,1:T(8,128)} %param.12) | copy-start | bytes 82948
  19.7 0.7 copy-start.6
  21.0 5.2 %collective-permute-start.4 = (f32[70,256]{1,0:T(8,128)S(1)}, f32[70,256]{1,0:T(8,128)S(1)}, u32[]{:S(2)}, u32[]{:S(2)}) collective-permute-start(f32[70,256]{1,0:T(8,128)S(1)} %get-tuple-element.46), channel_id=1, source_target_pairs={{0,1},{1,0},{2,3},{3,2},{4,5},{5,4},{6,7},{7,6},{8,9},{9,8},{10,11... | collective-permute-start | bytes 215048 | tf_op jit(solution)/shard_map/ppermute | solution.py:677
  23.2 4.0 %collective-permute-start.5 = (f32[70,256]{1,0:T(8,128)S(1)}, f32[70,256]{1,0:T(8,128)S(1)}, u32[]{:S(2)}, u32[]{:S(2)}) collective-permute-start(f32[70,256]{1,0:T(8,128)S(1)} %get-tuple-element.47), channel_id=1, source_target_pairs={{0,15},{1,2},{2,1},{3,4},{4,3},{5,6},{6,5},{7,8},{8,7},{9,10},{10,... | collective-permute-start | bytes 215048 | tf_op jit(solution)/shard_map/ppermute | solution.py:677
  24.6 0.8 %copy-start.3 = (f32[16,8,2,2,2]{0,4,3,2,1:T(2,128)S(1)}, f32[16,8,2,2,2]{0,4,3,2,1:T(2,128)}, u32[]{:S(2)}) copy-start(f32[16,8,2,2,2]{0,4,3,2,1:T(2,128)} %param.11) | copy-start | bytes 12292
  25.4 0.8 %copy-start.4 = (f32[8,16,2,2,2]{1,4,3,2,0:T(2,128)S(1)}, f32[8,16,2,2,2]{1,4,3,2,0:T(2,128)}, u32[]{:S(2)}) copy-start(f32[8,16,2,2,2]{1,4,3,2,0:T(2,128)} %param.13) | copy-start | bytes 12292
  26.1 1.1 %copy-start.1 = (f32[1,4,8,256]{3,2,1,0:T(8,128)S(1)}, f32[1,4,8,256]{3,2,1,0:T(8,128)}, u32[]{:S(2)}) copy-start(f32[1,4,8,256]{3,2,1,0:T(8,128)} %param.9) | copy-start | bytes 98308
  38.2 4.2 %collective-permute-start.6 = (f32[128,128]{1,0:T(8,128)S(1)}, f32[128,128]{1,0:T(8,128)S(1)}, u32[]{:S(2)}, u32[]{:S(2)}) collective-permute-start(f32[128,128]{1,0:T(8,128)S(1)} %get-tuple-element.57), channel_id=1, source_target_pairs={{0,1},{1,0},{2,3},{3,2},{4,5},{5,4},{6,7},{7,6},{8,9},{9,8},{10,11... | collective-permute-start | bytes 196616 | tf_op jit(solution)/shard_map/ppermute | solution.py:734
  40.6 3.7 %collective-permute-start.7 = (f32[128,128]{1,0:T(8,128)S(1)}, f32[128,128]{1,0:T(8,128)S(1)}, u32[]{:S(2)}, u32[]{:S(2)}) collective-permute-start(f32[128,128]{1,0:T(8,128)S(1)} %get-tuple-element.57), channel_id=1, source_target_pairs={{0,2},{1,3},{2,0},{3,1},{4,6},{5,7},{6,4},{7,5},{8,10},{9,11},{10,... | collective-permute-start | bytes 196616 | tf_op jit(solution)/shard_map/ppermute | solution.py:734
  40.6 5.2 %collective-permute-start.8 = (f32[128,128]{1,0:T(8,128)S(1)}, f32[128,128]{1,0:T(8,128)S(1)}, u32[]{:S(2)}, u32[]{:S(2)}) collective-permute-start(f32[128,128]{1,0:T(8,128)S(1)} %get-tuple-element.57), channel_id=1, source_target_pairs={{0,3},{1,2},{2,1},{3,0},{4,7},{5,6},{6,5},{7,4},{8,11},{9,10},{10,... | collective-permute-start | bytes 196616 | tf_op jit(solution)/shard_map/ppermute | solution.py:734
  45.9 4.4 %collective-permute-start.10 = (f32[64,128]{1,0:T(8,128)S(1)}, f32[64,128]{1,0:T(8,128)S(1)}, u32[]{:S(2)}, u32[]{:S(2)}) collective-permute-start(f32[64,128]{1,0:T(8,128)S(1)} %fusion), channel_id=1, source_target_pairs={{0,8},{1,9},{2,10},{3,11},{4,12},{5,13},{6,14},{7,15},{8,0},{9,1},... | collective-permute-start | bytes 98312 | tf_op jit(solution)/shard_map/ppermute | solution.py:734
  47.7 4.0 %collective-permute-start.11 = (f32[64,128]{1,0:T(8,128)S(1)}, f32[64,128]{1,0:T(8,128)S(1)}, u32[]{:S(2)}, u32[]{:S(2)}) collective-permute-start(f32[64,128]{1,0:T(8,128)S(1)} %fusion), channel_id=1, source_target_pairs={{0,12},{1,13},{2,14},{3,15},{4,8},{5,9},{6,10},{7,11},{8,4},{9,5},... | collective-permute-start | bytes 98312 | tf_op jit(solution)/shard_map/ppermute | solution.py:734
  48.7 2.9 %collective-permute-start.9 = (f32[64,128]{1,0:T(8,128)S(1)}, f32[64,128]{1,0:T(8,128)S(1)}, u32[]{:S(2)}, u32[]{:S(2)}) collective-permute-start(f32[64,128]{1,0:T(8,128)S(1)} %fusion), channel_id=1, source_target_pairs={{0,4},{1,5},{2,6},{3,7},{4,0},{5,1},{6,2},{7,3},{8,12},{9,13},{10,... | collective-permute-start | bytes 98312 | tf_op jit(solution)/shard_map/ppermute | solution.py:734
  51.7 4.0 %collective-permute-start.12 = (f32[64,128]{1,0:T(8,128)S(1)}, f32[64,128]{1,0:T(8,128)S(1)}, u32[]{:S(2)}, u32[]{:S(2)}) collective-permute-start(f32[64,128]{1,0:T(8,128)S(1)} %add_add_fusion.1), channel_id=1, source_target_pairs={{0,16},{16,0},{32,48},{48,32},{64,80},{80,64},{96,112},{112,96},{1... | collective-permute-start | bytes 98312 | tf_op jit(solution)/shard_map/ppermute | solution.py:734
  55.6 4.9 %collective-permute-start.13 = (f32[64,128]{1,0:T(8,128)S(1)}, f32[64,128]{1,0:T(8,128)S(1)}, u32[]{:S(2)}, u32[]{:S(2)}) collective-permute-start(f32[64,128]{1,0:T(8,128)S(1)} %add.55), channel_id=1, source_target_pairs={{0,48},{16,32},{32,16},{48,0},{64,112},{80,96},{96,80},{112,64},{1... | collective-permute-start | bytes 98312 | tf_op jit(solution)/shard_map/ppermute | solution.py:734
  60.5 3.9 %collective-permute-start.14 = (f32[64,128]{1,0:T(8,128)S(1)}, f32[64,128]{1,0:T(8,128)S(1)}, u32[]{:S(2)}, u32[]{:S(2)}) collective-permute-start(f32[64,128]{1,0:T(8,128)S(1)} %add.56), channel_id=1, source_target_pairs={{0,64},{16,80},{32,96},{48,112},{64,0},{80,16},{96,32},{112,48},{1... | collective-permute-start | bytes 98312 | tf_op jit(solution)/shard_map/ppermute | solution.py:734
  61.1 4.3 %collective-permute-start.15 = (f32[64,128]{1,0:T(8,128)S(1)}, f32[64,128]{1,0:T(8,128)S(1)}, u32[]{:S(2)}, u32[]{:S(2)}) collective-permute-start(f32[64,128]{1,0:T(8,128)S(1)} %add.56), channel_id=1, source_target_pairs={{0,128},{16,144},{32,160},{48,176},{64,192},{80,208},{96,224},{112... | collective-permute-start | bytes 98312 | tf_op jit(solution)/shard_map/ppermute | solution.py:734
  63.5 4.0 %collective-permute-start.16 = (f32[64,128]{1,0:T(8,128)S(1)}, f32[64,128]{1,0:T(8,128)S(1)}, u32[]{:S(2)}, u32[]{:S(2)}) collective-permute-start(f32[64,128]{1,0:T(8,128)S(1)} %add.56), channel_id=1, source_target_pairs={{0,192},{16,208},{32,224},{48,240},{64,128},{80,144},{96,160},{112... | collective-permute-start | bytes 98312 | tf_op jit(solution)/shard_map/ppermute | solution.py:734
  67.5 6.6 %collective-permute-start.17 = (f32[64,128]{1,0:T(8,128)S(1)}, f32[64,128]{1,0:T(8,128)S(1)}, u32[]{:S(2)}, u32[]{:S(2)}) collective-permute-start(f32[64,128]{1,0:T(8,128)S(1)} %add_add_fusion.mine), channel_id=1, source_target_pairs={{0,1},{1,0},{2,3},{3,2},{4,5},{5,4},{6,7},{7,6},{8,9},{9,8},{10,11... | collective-permute-start | bytes 98312 | tf_op jit(solution)/shard_map/ppermute | solution.py:741

commit v4 on v2

--- a/solution.py
+++ b/solution.py
@@ -724,7 +724,7 @@
     act_own, pay = run_kernel([pos, wide, *beside, cot, *weights], scale, size_x, size_y)
 
     blocks, imitated = [pay], None
-    for axis in ("gy", "gx"):
+    for axis in ("gx", "gy"):
         count = lax.axis_size(axis)
         for partners in rounds(count, axis == "gx"):
             while len(blocks) > 1:

time: 73.6 us -> 74.8 us (1.016)
  the two profiles are of different devices: /device:TPU:6 before, /device:TPU:2 now
where the time goes in v4:
time: 74.8 us; the launch traced here: 74.4 us
  starting transfers between devices  34.1 us (46%)
  waiting for transfers between devices  19.9 us (27%)
  Pallas kernels  13.5 us (18%)
  local copies, waits for them, and re-layouts  5.1 us (7%)
  other arithmetic  0.88 us (1%)
  between operations  0.84 us (1%)
    ppermute x11, waiting for transfers between devices, shards(): lax.ppermute(mine, axis, [(i, i ^ k) for i in range(count)])  19.3 us
    ppermute x3, starting transfers between devices, swap(): lax.ppermute(second, axis, pairs(1))  15.2 us
    ppermute x11, starting transfers between devices, shards(): lax.ppermute(mine, axis, [(i, i ^ k) for i in range(count)])  14.6 us
    pallas_call x1, Pallas kernels, run_kernel(): pl.pallas_call(unet_tile, out_shape=(jax.ShapeDtypeStruct((2, 128, 256),...  10.9 us
    ppermute x3, starting transfers between devices, swap(): lax.ppermute(first, axis, pairs(0))  4.31 us
    unnamed x18, local copies, waits for them, and re-layouts  3.77 us
  transfers between devices with their start and end apart: 17, of which 9 were waited for; matrix products, arithmetic and copies ran while one was open for 4% of the time, Pallas kernels for 2%

profile of v4, /device:TPU:2, one launch (start us, length us, event | category | flops | bytes accessed | tf_op | source)
XLA Modules:
  0.0 74.4 jit_solution(287451924688849165)
XLA Ops:
  0.6 0.0 copy-start
  0.7 0.8 %select_bitcast_fusion = (f32[1,8,256]{2,1,0:T(8,128)S(1)}, f32[1,8,256]{2,1,0:T(8,128)S(1)}) fusion(f32[1,4,8,256]{3,2,1,0:T(8,128)} %param.8, pred[]{:T(512)S(6)} %eq.3), kind=kLoop, calls=%fused_computation.2 | loop fusion | flops 4096 | bytes 32769 | tf_op jit(solution)/shard_map/jit(_where)/select_n | solution.py:710
  1.4 0.0 copy-done
  1.4 3.3 %collective-permute-start = (f32[4,8,256]{2,1,0:T(8,128)S(1)}, f32[4,8,256]{2,1,0:T(8,128)S(1)}, u32[]{:S(2)}, u32[]{:S(2)}) collective-permute-start(f32[4,8,256]{2,1,0:T(8,128)S(1)} %bitcast.30), channel_id=1, source_target_pairs={{0,16},{16,0},{32,48},{48,32},{64,80},{80,64},{96,112},{112,96},{1... | collective-permute-start | bytes 98312 | tf_op jit(solution)/shard_map/ppermute | solution.py:673
  4.7 4.5 %collective-permute-start.1 = (f32[4,8,256]{2,1,0:T(8,128)S(1)}, f32[4,8,256]{2,1,0:T(8,128)S(1)}, u32[]{:S(2)}, u32[]{:S(2)}) collective-permute-start(f32[4,8,256]{2,1,0:T(8,128)S(1)} %bitcast.31), channel_id=1, source_target_pairs={{0,240},{16,32},{32,16},{48,64},{64,48},{80,96},{96,80},{112,128},... | collective-permute-start | bytes 98312 | tf_op jit(solution)/shard_map/ppermute | solution.py:673
  9.1 0.9 %collective-permute-start.2 = (f32[1,8,256]{2,1,0:T(8,128)S(1)}, f32[1,8,256]{2,1,0:T(8,128)S(1)}, u32[]{:S(2)}, u32[]{:S(2)}) collective-permute-start(f32[1,8,256]{2,1,0:T(8,128)S(1)} %get-tuple-element.36), channel_id=1, source_target_pairs={{0,32},{16,48},{32,0},{48,16},{64,96},{80,112},{96,64},{112,80},{1... | collective-permute-start | bytes 24584 | tf_op jit(solution)/shard_map/ppermute | solution.py:673
  10.1 7.2 %collective-permute-start.3 = (f32[1,8,256]{2,1,0:T(8,128)S(1)}, f32[1,8,256]{2,1,0:T(8,128)S(1)}, u32[]{:S(2)}, u32[]{:S(2)}) collective-permute-start(f32[1,8,256]{2,1,0:T(8,128)S(1)} %get-tuple-element.37), channel_id=1, source_target_pairs={{0,224},{16,240},{32,64},{48,80},{64,32},{80,48},{96,128},{112,144... | collective-permute-start | bytes 24584 | tf_op jit(solution)/shard_map/ppermute | solution.py:673
  17.3 0.1 pad_add_fusion.pos.refs_0_
  17.3 1.0 %copy.21 = f32[27,8,16]{2,1,0:T(8,128)S(1)} copy(f32[27,8,16]{0,2,1:T(8,128)} %param.14) | data formatting | bytes 27648 | tf_op args[6]
  18.3 0.2 reshape.95
  18.5 0.1 copy.30
  18.6 0.1 pad.25.clone
  18.7 0.0 copy-start.5
  18.7 0.4 reshape.96.refs_9_
  19.1 0.3 copy-done.5
  19.4 0.1 copy.19
  19.5 0.2 copy.29
  19.7 0.0 copy-start.2
  19.7 0.0 copy-start.6
  19.7 0.1 reshape.94.refs_5_
  19.8 0.6 copy-done.6
  20.4 0.0 collective-permute-done.2.far_0
  20.4 0.0 collective-permute-done.3.far_1
  20.4 0.0 collective-permute-done.near_0
  20.4 0.0 collective-permute-done.1.near_1
  20.4 0.6 shard_map.135
  21.0 0.1 collective-permute-start.4
  21.1 3.6 %collective-permute-start.5 = (f32[70,256]{1,0:T(8,128)S(1)}, f32[70,256]{1,0:T(8,128)S(1)}, u32[]{:S(2)}, u32[]{:S(2)}) collective-permute-start(f32[70,256]{1,0:T(8,128)S(1)} %get-tuple-element.45), channel_id=1, source_target_pairs={{0,15},{1,2},{2,1},{3,4},{4,3},{5,6},{6,5},{7,8},{8,7},{9,10},{10,... | collective-permute-start | bytes 215048 | tf_op jit(solution)/shard_map/ppermute | solution.py:673
  24.7 0.0 copy-done.2
  24.7 0.2 copy.25
  24.8 0.1 copy.26
  25.0 0.2 reshape.100
  25.2 0.7 copy-done.3
  25.9 0.0 copy-start.4
  25.9 0.1 copy.28.refs_6_
  26.0 0.7 copy-done.4
  26.7 0.0 collective-permute-done.4.refs_2_
  26.7 0.6 collective-permute-done.5.refs_3_
  27.3 0.1 copy-done.1
  27.4 10.9 %shard_map.136 = (f32[2,128,256]{2,1,0:T(8,128)S(1)}, f32[120,128]{1,0:T(8,128)S(1)}) custom-call(s32[2]{0:T(128)S(1)} %pad_add_fusion.pos.refs_0_, f32[14,8,256]{2,1,0:T(8,128)S(1)} %get-tuple-element.43.refs_1_, f32[70,256]{1,0:T(8,128)S(1)} %collective-permute-done.4.refs_2_, f32[70,256]{1,0:T(8,128)S(1)} %collective-permute-done.5.refs_3_, ...), custom_call_target="tpu_custom_call" | custom-call | flops 3000000000 | bytes 2000000 | tf_op jit(solution)/shard_map/pallas_call | solution.py:656
  38.4 1.2 %collective-permute-start.6 = (f32[120,128]{1,0:T(8,128)S(1)}, f32[120,128]{1,0:T(8,128)S(1)}, u32[]{:S(2)}, u32[]{:S(2)}) collective-permute-start(f32[120,128]{1,0:T(8,128)S(1)} %get-tuple-element.55), channel_id=1, source_target_pairs={{0,16},{16,0},{32,48},{48,32},{64,80},{80,64},{96,112},{112,96},{1... | collective-permute-start | bytes 184328 | tf_op jit(solution)/shard_map/ppermute | solution.py:733
  39.5 4.1 %collective-permute-done.6 = f32[120,128]{1,0:T(8,128)S(1)} collective-permute-done((f32[120,128]{1,0:T(8,128)S(1)}, f32[120,128]{1,0:T(8,128)S(1)}, u32[]{:S(2)}, u32[]{:S(2)}) %collective-permute-start.6) | collective-permute-done | bytes 61472 | tf_op jit(solution)/shard_map/ppermute | solution.py:733
  43.6 2.4 %collective-permute-start.7 = (f32[120,128]{1,0:T(8,128)S(1)}, f32[120,128]{1,0:T(8,128)S(1)}, u32[]{:S(2)}, u32[]{:S(2)}) collective-permute-start(f32[120,128]{1,0:T(8,128)S(1)} %add.36), channel_id=1, source_target_pairs={{0,48},{16,32},{32,16},{48,0},{64,112},{80,96},{96,80},{112,64},{1... | collective-permute-start | bytes 184328 | tf_op jit(solution)/shard_map/ppermute | solution.py:733
  46.0 4.1 %collective-permute-done.7 = f32[120,128]{1,0:T(8,128)S(1)} collective-permute-done((f32[120,128]{1,0:T(8,128)S(1)}, f32[120,128]{1,0:T(8,128)S(1)}, u32[]{:S(2)}, u32[]{:S(2)}) %collective-permute-start.7) | collective-permute-done | bytes 61472 | tf_op jit(solution)/shard_map/ppermute | solution.py:733
  50.0 0.1 collective-permute-start.10
  50.1 2.6 %collective-permute-start.8 = (f32[120,128]{1,0:T(8,128)S(1)}, f32[120,128]{1,0:T(8,128)S(1)}, u32[]{:S(2)}, u32[]{:S(2)}) collective-permute-start(f32[120,128]{1,0:T(8,128)S(1)} %add.37), channel_id=1, source_target_pairs={{0,64},{16,80},{32,96},{48,112},{64,0},{80,16},{96,32},{112,48},{1... | collective-permute-start | bytes 184328 | tf_op jit(solution)/shard_map/ppermute | solution.py:733
  52.8 0.8 %collective-permute-start.9 = (f32[120,128]{1,0:T(8,128)S(1)}, f32[120,128]{1,0:T(8,128)S(1)}, u32[]{:S(2)}, u32[]{:S(2)}) collective-permute-start(f32[120,128]{1,0:T(8,128)S(1)} %add.37), channel_id=1, source_target_pairs={{0,128},{16,144},{32,160},{48,176},{64,192},{80,208},{96,224},{112... | collective-permute-start | bytes 184328 | tf_op jit(solution)/shard_map/ppermute | solution.py:733
  53.6 0.7 collective-permute-done.10
  54.4 0.6 collective-permute-done.8
  55.0 3.5 %collective-permute-done.9 = f32[120,128]{1,0:T(8,128)S(1)} collective-permute-done((f32[120,128]{1,0:T(8,128)S(1)}, f32[120,128]{1,0:T(8,128)S(1)}, u32[]{:S(2)}, u32[]{:S(2)}) %collective-permute-start.9) | collective-permute-done | bytes 61472 | tf_op jit(solution)/shard_map/ppermute | solution.py:733
  58.5 0.1 collective-permute-start.11
  58.6 0.3 collective-permute-start.12
  58.9 1.5 %collective-permute-start.13 = (f32[120,128]{1,0:T(8,128)S(1)}, f32[120,128]{1,0:T(8,128)S(1)}, u32[]{:S(2)}, u32[]{:S(2)}) collective-permute-start(f32[120,128]{1,0:T(8,128)S(1)} %add_add_fusion.1), channel_id=1, source_target_pairs={{0,3},{1,2},{2,1},{3,0},{4,7},{5,6},{6,5},{7,4},{8,11},{9,10},{10,... | collective-permute-start | bytes 184328 | tf_op jit(solution)/shard_map/ppermute | solution.py:733
  60.5 0.0 collective-permute-done.11
  60.5 3.2 %collective-permute-done.12 = f32[120,128]{1,0:T(8,128)S(1)} collective-permute-done((f32[120,128]{1,0:T(8,128)S(1)}, f32[120,128]{1,0:T(8,128)S(1)}, u32[]{:S(2)}, u32[]{:S(2)}) %collective-permute-start.12) | collective-permute-done | bytes 61472 | tf_op jit(solution)/shard_map/ppermute | solution.py:733
  63.7 0.0 collective-permute-done.13
  63.7 2.8 %collective-permute-start.14 = (f32[120,128]{1,0:T(8,128)S(1)}, f32[120,128]{1,0:T(8,128)S(1)}, u32[]{:S(2)}, u32[]{:S(2)}) collective-permute-start(f32[120,128]{1,0:T(8,128)S(1)} %add_add_fusion.refs_0_), channel_id=1, source_target_pairs={{0,4},{1,5},{2,6},{3,7},{4,0},{5,1},{6,2},{7,3},{8,12},{9,13},{10,... | collective-permute-start | bytes 184328 | tf_op jit(solution)/shard_map/ppermute | solution.py:733
  66.5 1.6 %collective-permute-start.15 = (f32[120,128]{1,0:T(8,128)S(1)}, f32[120,128]{1,0:T(8,128)S(1)}, u32[]{:S(2)}, u32[]{:S(2)}) collective-permute-start(f32[120,128]{1,0:T(8,128)S(1)} %add_add_fusion.refs_0_), channel_id=1, source_target_pairs={{0,8},{1,9},{2,10},{3,11},{4,12},{5,13},{6,14},{7,15},{8,0},{9,1},... | collective-permute-start | bytes 184328 | tf_op jit(solution)/shard_map/ppermute | solution.py:733
  68.1 1.1 %collective-permute-start.16 = (f32[120,128]{1,0:T(8,128)S(1)}, f32[120,128]{1,0:T(8,128)S(1)}, u32[]{:S(2)}, u32[]{:S(2)}) collective-permute-start(f32[120,128]{1,0:T(8,128)S(1)} %add_add_fusion.refs_0_), channel_id=1, source_target_pairs={{0,12},{1,13},{2,14},{3,15},{4,8},{5,9},{6,10},{7,11},{8,4},{9,5},... | collective-permute-start | bytes 184328 | tf_op jit(solution)/shard_map/ppermute | solution.py:733
  69.3 1.2 %shard_map.137 = f32[4,8,256]{2,1,0:T(8,128)} custom-call(f32[2,128,256]{2,1,0:T(8,128)S(1)} %get-tuple-element.54.act_own, f32[1,128]{1,0:T(1,128)S(1)} %pad.26.refs_10_.w_last), custom_call_target="tpu_custom_call" | custom-call | flops 200000000 | bytes 400000 | tf_op jit(solution)/shard_map/pallas_call | solution.py:564
  70.4 0.0 collective-permute-done.14.refs_1_
  70.4 1.8 %collective-permute-done.15.refs_2_ = f32[120,128]{1,0:T(8,128)S(1)} collective-permute-done((f32[120,128]{1,0:T(8,128)S(1)}, f32[120,128]{1,0:T(8,128)S(1)}, u32[]{:S(2)}, u32[]{:S(2)}) %collective-permute-start.15) | collective-permute-done | bytes 61472 | tf_op jit(solution)/shard_map/ppermute | solution.py:733
  72.3 1.3 %collective-permute-done.16.refs_3_ = f32[120,128]{1,0:T(8,128)S(1)} collective-permute-done((f32[120,128]{1,0:T(8,128)S(1)}, f32[120,128]{1,0:T(8,128)S(1)}, u32[]{:S(2)}, u32[]{:S(2)}) %collective-permute-start.16) | collective-permute-done | bytes 61472 | tf_op jit(solution)/shard_map/ppermute | solution.py:733
  73.5 0.8 %shard_map.138 = (f32[16,16,27]{2,1,0:T(8,128)}, f32[8,16,27]{2,1,0:T(8,128)}, f32[8,1,27]{2,1,0:T(1,128)}, f32[8,4,2,16]{3,2,1,0:T(2,128)}, f32[8,4,2,16]{3,2,1,0:T(2,128)}, /*index=5*/f32[1,8]{1,0:T(1,128)}) custom-call(f32[120,128]{1,0:T(8,128)S(1)} %add_add_fusion.refs_0_, f32[120,128]{1,0:T(8,128)S(1)} %collective-permute-done.14.refs_1_, ...), custom_call_target="tpu_custom_call" | custom-call | tf_op jit(solution)/shard_map/pallas_call | solution.py:614
  (14 shorter events, 0.1 us)
Async XLA Ops:
  0.6 0.8 %copy-start = (f32[1,4,8,256]{3,2,1,0:T(8,128)S(1)}, f32[1,4,8,256]{3,2,1,0:T(8,128)}, u32[]{:S(2)}) copy-start(f32[1,4,8,256]{3,2,1,0:T(8,128)} %param.8) | copy-start | bytes 98308
  1.4 19.0 %collective-permute-start = (f32[4,8,256]{2,1,0:T(8,128)S(1)}, f32[4,8,256]{2,1,0:T(8,128)S(1)}, u32[]{:S(2)}, u32[]{:S(2)}) collective-permute-start(f32[4,8,256]{2,1,0:T(8,128)S(1)} %bitcast.30), channel_id=1, source_target_pairs={{0,16},{16,0},{32,48},{48,32},{64,80},{80,64},{96,112},{112,96},{1... | collective-permute-start | bytes 98312 | tf_op jit(solution)/shard_map/ppermute | solution.py:673
  4.7 15.7 %collective-permute-start.1 = (f32[4,8,256]{2,1,0:T(8,128)S(1)}, f32[4,8,256]{2,1,0:T(8,128)S(1)}, u32[]{:S(2)}, u32[]{:S(2)}) collective-permute-start(f32[4,8,256]{2,1,0:T(8,128)S(1)} %bitcast.31), channel_id=1, source_target_pairs={{0,240},{16,32},{32,16},{48,64},{64,48},{80,96},{96,80},{112,128},... | collective-permute-start | bytes 98312 | tf_op jit(solution)/shard_map/ppermute | solution.py:673
  9.1 11.2 %collective-permute-start.2 = (f32[1,8,256]{2,1,0:T(8,128)S(1)}, f32[1,8,256]{2,1,0:T(8,128)S(1)}, u32[]{:S(2)}, u32[]{:S(2)}) collective-permute-start(f32[1,8,256]{2,1,0:T(8,128)S(1)} %get-tuple-element.36), channel_id=1, source_target_pairs={{0,32},{16,48},{32,0},{48,16},{64,96},{80,112},{96,64},{112,80},{1... | collective-permute-start | bytes 24584 | tf_op jit(solution)/shard_map/ppermute | solution.py:673
  10.1 10.3 %collective-permute-start.3 = (f32[1,8,256]{2,1,0:T(8,128)S(1)}, f32[1,8,256]{2,1,0:T(8,128)S(1)}, u32[]{:S(2)}, u32[]{:S(2)}) collective-permute-start(f32[1,8,256]{2,1,0:T(8,128)S(1)} %get-tuple-element.37), channel_id=1, source_target_pairs={{0,224},{16,240},{32,64},{48,80},{64,32},{80,48},{96,128},{112,144... | collective-permute-start | bytes 24584 | tf_op jit(solution)/shard_map/ppermute | solution.py:673
  18.7 0.7 copy-start.5
  19.7 5.0 %copy-start.2 = (f32[27,16,16]{0,2,1:T(8,128)S(1)}, f32[27,16,16]{0,2,1:T(8,128)}, u32[]{:S(2)}) copy-start(f32[27,16,16]{0,2,1:T(8,128)} %param.12) | copy-start | bytes 82948
  19.7 0.7 copy-start.6
  21.0 5.7 %collective-permute-start.4 = (f32[70,256]{1,0:T(8,128)S(1)}, f32[70,256]{1,0:T(8,128)S(1)}, u32[]{:S(2)}, u32[]{:S(2)}) collective-permute-start(f32[70,256]{1,0:T(8,128)S(1)} %get-tuple-element.44), channel_id=1, source_target_pairs={{0,1},{1,0},{2,3},{3,2},{4,5},{5,4},{6,7},{7,6},{8,9},{9,8},{10,11... | collective-permute-start | bytes 215048 | tf_op jit(solution)/shard_map/ppermute | solution.py:673
  21.1 6.2 %collective-permute-start.5 = (f32[70,256]{1,0:T(8,128)S(1)}, f32[70,256]{1,0:T(8,128)S(1)}, u32[]{:S(2)}, u32[]{:S(2)}) collective-permute-start(f32[70,256]{1,0:T(8,128)S(1)} %get-tuple-element.45), channel_id=1, source_target_pairs={{0,15},{1,2},{2,1},{3,4},{4,3},{5,6},{6,5},{7,8},{8,7},{9,10},{10,... | collective-permute-start | bytes 215048 | tf_op jit(solution)/shard_map/ppermute | solution.py:673
  25.1 0.8 %copy-start.3 = (f32[16,8,2,2,2]{0,4,3,2,1:T(2,128)S(1)}, f32[16,8,2,2,2]{0,4,3,2,1:T(2,128)}, u32[]{:S(2)}) copy-start(f32[16,8,2,2,2]{0,4,3,2,1:T(2,128)} %param.11) | copy-start | bytes 12292
  25.9 0.8 %copy-start.4 = (f32[8,16,2,2,2]{1,4,3,2,0:T(2,128)S(1)}, f32[8,16,2,2,2]{1,4,3,2,0:T(2,128)}, u32[]{:S(2)}) copy-start(f32[8,16,2,2,2]{1,4,3,2,0:T(2,128)} %param.13) | copy-start | bytes 12292
  26.7 0.8 %copy-start.1 = (f32[1,4,8,256]{3,2,1,0:T(8,128)S(1)}, f32[1,4,8,256]{3,2,1,0:T(8,128)}, u32[]{:S(2)}) copy-start(f32[1,4,8,256]{3,2,1,0:T(8,128)} %param.9) | copy-start | bytes 98308
  38.4 5.2 %collective-permute-start.6 = (f32[120,128]{1,0:T(8,128)S(1)}, f32[120,128]{1,0:T(8,128)S(1)}, u32[]{:S(2)}, u32[]{:S(2)}) collective-permute-start(f32[120,128]{1,0:T(8,128)S(1)} %get-tuple-element.55), channel_id=1, source_target_pairs={{0,16},{16,0},{32,48},{48,32},{64,80},{80,64},{96,112},{112,96},{1... | collective-permute-start | bytes 184328 | tf_op jit(solution)/shard_map/ppermute | solution.py:733
  43.6 6.4 %collective-permute-start.7 = (f32[120,128]{1,0:T(8,128)S(1)}, f32[120,128]{1,0:T(8,128)S(1)}, u32[]{:S(2)}, u32[]{:S(2)}) collective-permute-start(f32[120,128]{1,0:T(8,128)S(1)} %add.36), channel_id=1, source_target_pairs={{0,48},{16,32},{32,16},{48,0},{64,112},{80,96},{96,80},{112,64},{1... | collective-permute-start | bytes 184328 | tf_op jit(solution)/shard_map/ppermute | solution.py:733
  50.0 4.3 %collective-permute-start.10 = (f32[120,128]{1,0:T(8,128)S(1)}, f32[120,128]{1,0:T(8,128)S(1)}, u32[]{:S(2)}, u32[]{:S(2)}) collective-permute-start(f32[120,128]{1,0:T(8,128)S(1)} %add.37), channel_id=1, source_target_pairs={{0,192},{16,208},{32,224},{48,240},{64,128},{80,144},{96,160},{112... | collective-permute-start | bytes 184328 | tf_op jit(solution)/shard_map/ppermute | solution.py:733
  50.1 4.8 %collective-permute-start.8 = (f32[120,128]{1,0:T(8,128)S(1)}, f32[120,128]{1,0:T(8,128)S(1)}, u32[]{:S(2)}, u32[]{:S(2)}) collective-permute-start(f32[120,128]{1,0:T(8,128)S(1)} %add.37), channel_id=1, source_target_pairs={{0,64},{16,80},{32,96},{48,112},{64,0},{80,16},{96,32},{112,48},{1... | collective-permute-start | bytes 184328 | tf_op jit(solution)/shard_map/ppermute | solution.py:733
  52.8 5.7 %collective-permute-start.9 = (f32[120,128]{1,0:T(8,128)S(1)}, f32[120,128]{1,0:T(8,128)S(1)}, u32[]{:S(2)}, u32[]{:S(2)}) collective-permute-start(f32[120,128]{1,0:T(8,128)S(1)} %add.37), channel_id=1, source_target_pairs={{0,128},{16,144},{32,160},{48,176},{64,192},{80,208},{96,224},{112... | collective-permute-start | bytes 184328 | tf_op jit(solution)/shard_map/ppermute | solution.py:733
  58.5 2.0 %collective-permute-start.11 = (f32[120,128]{1,0:T(8,128)S(1)}, f32[120,128]{1,0:T(8,128)S(1)}, u32[]{:S(2)}, u32[]{:S(2)}) collective-permute-start(f32[120,128]{1,0:T(8,128)S(1)} %add_add_fusion.1), channel_id=1, source_target_pairs={{0,1},{1,0},{2,3},{3,2},{4,5},{5,4},{6,7},{7,6},{8,9},{9,8},{10,11... | collective-permute-start | bytes 184328 | tf_op jit(solution)/shard_map/ppermute | solution.py:733
  58.6 5.1 %collective-permute-start.12 = (f32[120,128]{1,0:T(8,128)S(1)}, f32[120,128]{1,0:T(8,128)S(1)}, u32[]{:S(2)}, u32[]{:S(2)}) collective-permute-start(f32[120,128]{1,0:T(8,128)S(1)} %add_add_fusion.1), channel_id=1, source_target_pairs={{0,2},{1,3},{2,0},{3,1},{4,6},{5,7},{6,4},{7,5},{8,10},{9,11},{10,... | collective-permute-start | bytes 184328 | tf_op jit(solution)/shard_map/ppermute | solution.py:733
  58.9 4.7 %collective-permute-start.13 = (f32[120,128]{1,0:T(8,128)S(1)}, f32[120,128]{1,0:T(8,128)S(1)}, u32[]{:S(2)}, u32[]{:S(2)}) collective-permute-start(f32[120,128]{1,0:T(8,128)S(1)} %add_add_fusion.1), channel_id=1, source_target_pairs={{0,3},{1,2},{2,1},{3,0},{4,7},{5,6},{6,5},{7,4},{8,11},{9,10},{10,... | collective-permute-start | bytes 184328 | tf_op jit(solution)/shard_map/ppermute | solution.py:733
  63.7 6.7 %collective-permute-start.14 = (f32[120,128]{1,0:T(8,128)S(1)}, f32[120,128]{1,0:T(8,128)S(1)}, u32[]{:S(2)}, u32[]{:S(2)}) collective-permute-start(f32[120,128]{1,0:T(8,128)S(1)} %add_add_fusion.refs_0_), channel_id=1, source_target_pairs={{0,4},{1,5},{2,6},{3,7},{4,0},{5,1},{6,2},{7,3},{8,12},{9,13},{10,... | collective-permute-start | bytes 184328 | tf_op jit(solution)/shard_map/ppermute | solution.py:733
  66.5 5.8 %collective-permute-start.15 = (f32[120,128]{1,0:T(8,128)S(1)}, f32[120,128]{1,0:T(8,128)S(1)}, u32[]{:S(2)}, u32[]{:S(2)}) collective-permute-start(f32[120,128]{1,0:T(8,128)S(1)} %add_add_fusion.refs_0_), channel_id=1, source_target_pairs={{0,8},{1,9},{2,10},{3,11},{4,12},{5,13},{6,14},{7,15},{8,0},{9,1},... | collective-permute-start | bytes 184328 | tf_op jit(solution)/shard_map/ppermute | solution.py:733
  68.1 5.4 %collective-permute-start.16 = (f32[120,128]{1,0:T(8,128)S(1)}, f32[120,128]{1,0:T(8,128)S(1)}, u32[]{:S(2)}, u32[]{:S(2)}) collective-permute-start(f32[120,128]{1,0:T(8,128)S(1)} %add_add_fusion.refs_0_), channel_id=1, source_target_pairs={{0,12},{1,13},{2,14},{3,15},{4,8},{5,9},{6,10},{7,11},{8,4},{9,5},... | collective-permute-start | bytes 184328 | tf_op jit(solution)/shard_map/ppermute | solution.py:733
